TPU v7x, 256 devices: a whole 4x4x8 slice. The times are simulated.
256 devices in a mesh: rep: 64 (over x, z, core), fsdp: 4 (over y).
Axes of the slice: x: 4, y: 4, z: 8, core: 2. Of those that a mesh axis runs over, the one named last changes fastest.
Arguments:
- grads: bfloat16 [64, 128, 27648], P('rep', None, 'fsdp')
- momentum: float32 [64, 128, 27648], P('rep', None, 'fsdp'), may hold values from -6 to 6
- master: float32 [128, 27648], P(None, 'fsdp'), may hold values from -6 to 6
- band_index: int32 [64, 2, 6912], P(None, None, 'fsdp'), may hold values from 0 to 4095, as said below
Outputs:
- new_momentum: float32 [64, 128, 27648], P('rep', None, 'fsdp')
- update: float32 [128, 27648], P(None, 'fsdp')
- weights_full: bfloat16 [128, 27648], replicated
Inputs may be any that keep to these rules, and one draw needn't show every extreme that they name: `band_index`: the j-th index of each block lies in [j * 64 * 4, (j + 1) * 64 * 4), so a block's indices are distinct.
All inputs are finite; a program needn't handle non-finite values.
Results may differ from a plain program's by a relative error of at most 0.001.
Values may be sent and summed in bfloat16 or wider, within the bound.
A program may use at most 128 MiB of HBM per device.

v0:
```python
import functools

import jax
import jax.numpy as jnp
import numpy as np
import ml_dtypes
from jax import lax
from jax.experimental import pallas as pl
from jax.experimental.pallas import tpu as pltpu
from jax.sharding import PartitionSpec as P

BLOCK = 64
BAND = 16
GROUP = 256
PER_STEP = 3

momentum_decay = 0.9
learn_rate = 0.05

bf16 = jnp.bfloat16
f32 = jnp.float32


def dct64():
    k = np.arange(BLOCK, dtype=np.float64)[:, None]
    n = np.arange(BLOCK, dtype=np.float64)[None, :]
    basis = np.cos(np.pi * (2.0 * n + 1.0) * k / (2.0 * BLOCK))
    return basis * np.where(k == 0.0, np.sqrt(1.0 / BLOCK), np.sqrt(2.0 / BLOCK))


def halves(table):
    hi = table.astype(np.float32).astype(ml_dtypes.bfloat16)
    lo = (table - hi.astype(np.float64)).astype(np.float32).astype(ml_dtypes.bfloat16)
    return hi, lo


def left_pair(table):
    hi, lo = halves(table)
    return np.concatenate([hi, hi], axis=1), lo


def make_tables():
    c = dct64()
    right = np.kron(np.eye(4), c.T)
    left = np.kron(np.eye(2), c)
    m, i = np.divmod(np.arange(BLOCK), 8)
    k1 = 4 * (m + 8 * (i // 4)) + i % 4
    back_perm = np.kron(np.eye(2), c[k1].T)
    spread = np.kron(np.eye(4), np.ones((BAND, BLOCK)))
    ones = np.kron(np.eye(4), np.ones((BLOCK, BLOCK)))
    as_bf16 = lambda a: a.astype(ml_dtypes.bfloat16)
    return dict(
        right=halves(right),
        right_t=halves(right.T),
        left=left_pair(left),
        left_t=left_pair(left.T),
        back=left_pair(back_perm),
        spread=as_bf16(spread),
        ones=as_bf16(ones),
    )


TABLES = make_tables()


def split(x):
    hi = x.astype(bf16)
    return hi, (x - hi.astype(f32)).astype(bf16)


def dot(a, b):
    return jnp.dot(a, b, preferred_element_type=f32)


def dot_nt(a, b):
    return lax.dot_general(a, b, (((1,), (1,)), ((), ())), preferred_element_type=f32)


def times_right(x, hi_ref, lo_ref):
    hi, lo = split(x)
    return dot(hi, hi_ref[...]) + (dot(lo, hi_ref[...]) + dot(hi, lo_ref[...]))


def times_left(pair_ref, lo_ref, x):
    hi, lo = split(x)
    return dot(pair_ref[...], jnp.concatenate([hi, lo], axis=0)) + dot(lo_ref[...], hi)


def local_kernel(
    own_ref, grads_ref, mom_ref, index_ref,
    r_hi, r_lo, rt_hi, rt_lo, l_pair, l_lo, lt_pair, lt_lo, spread_ref,
    fresh_ref, band_ref, wide,
):
    step = pl.program_id(0)
    groups = wide.shape[0]

    @pl.when(step == 0)
    def _():
        row = lax.broadcasted_iota(jnp.int32, (BLOCK, groups * BLOCK), 0)
        lane = lax.broadcasted_iota(jnp.int32, (BLOCK, groups * BLOCK), 1)
        mine = (lane & (BAND - 1)) == (row >> 2)
        for p in range(2):
            within = index_ref[0, p : p + 1, :] & 255
            placed = jnp.where(mine, jnp.broadcast_to(within, mine.shape), 0).astype(f32)
            for g in range(groups):
                wide[g, p * BLOCK : (p + 1) * BLOCK, :] = placed[:, g * BLOCK : (g + 1) * BLOCK].astype(bf16)

    row = lax.broadcasted_iota(jnp.int32, (2 * BLOCK, GROUP), 0)
    lane = lax.broadcasted_iota(jnp.int32, (2 * BLOCK, GROUP), 1)
    place = (((row & 3) << 6) + (lane & 63)).astype(f32)
    zrow = lax.broadcasted_iota(jnp.int32, (2 * BLOCK, BLOCK), 0)
    zlane = lax.broadcasted_iota(jnp.int32, (2 * BLOCK, BLOCK), 1)
    zmine = (zlane & (BAND - 1)) == ((zrow & 63) >> 2)
    for g in range(PER_STEP):
        cols = slice(g * GROUP, (g + 1) * GROUP)
        acc = momentum_decay * mom_ref[0, :, cols] + grads_ref[0, :, cols].astype(f32)
        coeff = times_left(l_pair, l_lo, times_right(acc, r_hi, r_lo))
        index = dot(wide[step * PER_STEP + g], spread_ref[...])
        kept = jnp.where(index == place, coeff, 0.0)
        hi, mid = split(kept)
        low = (kept - hi.astype(f32) - mid.astype(f32)).astype(bf16)
        sums = dot_nt(hi, spread_ref[...]) + (dot_nt(mid, spread_ref[...]) + dot_nt(low, spread_ref[...]))
        sums = jnp.where(zmine, sums, 0.0)
        top = jnp.sum(sums[:BLOCK], axis=0, keepdims=True)
        bottom = jnp.sum(sums[BLOCK:], axis=0, keepdims=True)
        band_ref[:, g * 128 : (g + 1) * 128] = jnp.concatenate([top, bottom], axis=1)
        back = times_left(lt_pair, lt_lo, times_right(kept, rt_hi, rt_lo))
        fresh_ref[0, :, cols] = acc - back


def full(shape):
    return pl.BlockSpec(shape, lambda *_: (0,) * len(shape))


def local_part(own, grads, momentum, band_index):
    cols = grads.shape[2]
    groups = cols // GROUP
    steps = groups // PER_STEP
    width = PER_STEP * GROUP
    t = TABLES
    consts = [*t["right"], *t["right_t"], *t["left"], *t["left_t"], t["spread"]]
    slab = pl.BlockSpec((1, 2 * BLOCK, width), lambda s, own: (0, 0, s))
    return pl.pallas_call(
        local_kernel,
        grid_spec=pltpu.PrefetchScalarGridSpec(
            num_scalar_prefetch=1,
            grid=(steps,),
            in_specs=[slab, slab, pl.BlockSpec((1, 2, band_index.shape[2]), lambda s, own: (own[0], 0, 0))]
            + [full(c.shape) for c in consts],
            out_specs=[slab, pl.BlockSpec((1, PER_STEP * 128), lambda s, own: (0, s))],
            scratch_shapes=[pltpu.VMEM((groups, 2 * BLOCK, BLOCK), bf16)],
        ),
        out_shape=[
            jax.ShapeDtypeStruct(grads.shape, f32),
            jax.ShapeDtypeStruct((1, groups * 128), f32),
        ],
        compiler_params=pltpu.CompilerParams(vmem_limit_bytes=32 * 2**20),
    )(own, grads, momentum, band_index, *[jnp.asarray(c) for c in consts])


def summed_coefficients(band, index):
    reps = band.shape[0]
    band_t = band.T
    within = index.T & 255
    half = jnp.where(lax.broadcasted_iota(jnp.int32, (8, 2 * reps), 1) >= reps, 4, 0)
    eight = lax.broadcasted_iota(jnp.int32, (8, 2 * reps), 0)
    k2_of = lax.broadcasted_iota(jnp.int32, (BLOCK, 2 * reps), 0)
    zero = jnp.zeros((8, 2 * reps), f32)
    quarter = lax.broadcasted_iota(jnp.int32, (16, GROUP), 1) >> 6
    parts = []
    for p in range(2):
        values, codes, places = [], [], []
        for q in range(4):
            base = p * 64 + q * 16
            join = lambda x: jnp.concatenate([x[base : base + 8], x[base + 8 : base + 16]], axis=1)
            w = join(within)
            values.append(join(band_t))
            codes.append((w >> 6) + half)
            places.append(w & 63)
        for t in range(4):
            his, los, hots = [], [], []
            for q in range(4):
                a, b = [], []
                for m in (2 * t, 2 * t + 1):
                    spread = lambda x: jnp.broadcast_to(x[m : m + 1], eight.shape)
                    a.append(jnp.where(spread(codes[q]) == eight, spread(values[q]), 0.0))
                    here = jnp.broadcast_to(places[q][m : m + 1], k2_of.shape) == k2_of
                    b.append(jnp.where(here, 1.0, 0.0).astype(bf16))
                left = jnp.concatenate(
                    [jnp.concatenate([a[0], zero], axis=1), jnp.concatenate([zero, a[1]], axis=1)], axis=0
                )
                hi, lo = split(left)
                his.append(hi)
                los.append(lo)
                hots.append(jnp.concatenate(b, axis=1))
            out = dot_nt(jnp.concatenate(his + los, axis=0), jnp.concatenate(hots, axis=0))
            out = out[:64] + out[64:]
            rows = jnp.where(quarter == 0, out[:16], 0.0)
            for q in range(1, 4):
                rows = jnp.where(quarter == q, out[16 * q : 16 * (q + 1)], rows)
            parts.append(rows)
    return jnp.concatenate(parts, axis=0)


def shared_group(band, index, master, rt_hi, rt_lo, b_pair, b_lo, ones_ref):
    total = summed_coefficients(band, index)
    direction = times_left(b_pair, b_lo, times_right(total, rt_hi, rt_lo))
    square = direction * direction
    sums = [
        jnp.broadcast_to(jnp.sum(square[p * BLOCK : (p + 1) * BLOCK], axis=0, keepdims=True), (8, GROUP))
        for p in range(2)
    ]
    hi, lo = split(jnp.concatenate(sums, axis=0))
    means = (dot(hi, ones_ref[...]) + dot(lo, ones_ref[...])) * (1.0 / (BLOCK * BLOCK))
    scale = 0.1 * jnp.sqrt(means + 1e-06)
    scale = jnp.concatenate(
        [jnp.broadcast_to(scale[8 * p : 8 * p + 1], (BLOCK, GROUP)) for p in range(2)], axis=0
    )
    update = direction / (jnp.abs(direction) + scale)
    return update, (master - learn_rate * update).astype(bf16)


def shared_kernel(band_ref, index_ref, master_ref, rt_hi, rt_lo, b_pair, b_lo, ones_ref, update_ref, weights_ref):
    for g in range(PER_STEP):
        lanes = slice(g * 128, (g + 1) * 128)
        cols = slice(g * GROUP, (g + 1) * GROUP)
        update, weights = shared_group(
            band_ref[:, lanes], index_ref[:, lanes], master_ref[:, cols], rt_hi, rt_lo, b_pair, b_lo, ones_ref
        )
        update_ref[:, cols] = update
        weights_ref[:, cols] = weights


def shared_part(bands, index, master):
    reps = bands.shape[0]
    rows, cols = master.shape
    steps = cols // (GROUP * PER_STEP)
    t = TABLES
    consts = [*t["right_t"], *t["back"], t["ones"]]
    slab = pl.BlockSpec((rows, PER_STEP * GROUP), lambda s: (0, s))
    lanes = pl.BlockSpec((reps, PER_STEP * 128), lambda s: (0, s))
    return pl.pallas_call(
        shared_kernel,
        grid=(steps,),
        in_specs=[lanes, lanes, slab] + [full(c.shape) for c in consts],
        out_specs=[slab, slab],
        out_shape=[jax.ShapeDtypeStruct(master.shape, f32), jax.ShapeDtypeStruct(master.shape, bf16)],
        compiler_params=pltpu.CompilerParams(vmem_limit_bytes=32 * 2**20),
    )(bands, index, master, *[jnp.asarray(c) for c in consts])


def by_group(band_index):
    reps, _, lanes = band_index.shape
    split_up = band_index.reshape(reps, 2, lanes // BLOCK, BLOCK)
    return split_up.transpose(0, 2, 1, 3).reshape(reps, 2 * lanes)


def shards(grads, momentum, master, band_index):
    own = lax.axis_index("rep").astype(jnp.int32)[None]
    fresh, band = local_part(own, grads, momentum, band_index)
    bands = lax.all_gather(band, "rep", axis=0, tiled=True)
    update, weights_local = shared_part(bands, by_group(band_index), master)
    weights_full = lax.all_gather(weights_local, "fsdp", axis=1, tiled=True)
    return (fresh, update, weights_full)


def solution(mesh):
    in_specs = (
        P("rep", None, "fsdp"),
        P("rep", None, "fsdp"),
        P(None, "fsdp"),
        P(None, None, "fsdp"),
    )
    out_specs = (P("rep", None, "fsdp"), P(None, "fsdp"), P())
    return jax.shard_map(shards, mesh=mesh, in_specs=in_specs, out_specs=out_specs, check_vma=False)
```

profile of v0, /device:TPU:1, one launch (start us, length us, event | category | flops | bytes accessed | tf_op | source)
XLA Modules:
  0.0 209.9 jit_solution(11256326044371517972)
XLA Ops:
  7.2 0.0 all-gather.3.cloned.1.call-start
  7.2 1.2 copy.22
  8.5 2.1 reshape.12
  10.6 0.0 copy-start
  10.6 0.0 copy-start.5
  10.6 0.0 copy-start.6
  10.6 0.0 copy-start.8
  10.6 0.0 copy-start.9
  10.6 0.0 copy-start.11
  10.6 0.0 copy-start.12
  10.6 0.0 copy-start.14
  10.6 0.0 copy-start.15
  10.6 0.0 copy-start.16
  10.6 4.5 %copy.23 = s32[64,27,2,64]{3,2,1,0:T(2,128)} copy(s32[64,27,2,64]{3,1,0,2:T(8,128)} %bitcast.10) | data formatting | bytes 1769472 | tf_op jit(solution)/shard_map/transpose | solution.py:255
  15.2 2.6 %reshape.13.index_ref = s32[64,3456]{1,0:T(8,128)S(1)} reshape(s32[64,27,2,64]{3,2,1,0:T(2,128)} %copy.23) | data formatting | bytes 1769472 | tf_op jit(solution)/shard_map/reshape | solution.py:255
  17.8 0.0 copy-done
  17.8 0.0 copy-done.5
  17.8 0.0 copy-done.6
  17.8 0.0 copy-done.8
  17.8 0.0 copy-done.9
  17.8 0.0 copy-done.11
  17.8 0.0 copy-done.12
  17.8 0.0 copy-done.14
  17.8 0.0 copy-done.15
  17.8 0.0 copy-done.16
  17.9 0.0 copy-start.1
  17.9 2.0 copy-done.1
  19.9 0.0 copy-start.3
  19.9 1.5 copy-done.3
  21.3 0.0 copy-start.2
  21.3 0.0 copy-start.7
  21.3 0.0 copy-start.10
  21.3 0.0 copy-start.13
  21.4 18.2 %shard_map.175 = (f32[1,128,6912]{2,1,0:T(8,128)}, f32[1,3456]{1,0:T(1,128)S(1)}) custom-call(s32[1]{0:T(128)} %bitcast.own_ref, bf16[1,128,6912]{2,1,0:T(8,128)(2,1)S(1)} %copy-done.3, f32[1,128,6912]{2,1,0:T(8,128)S(1)} %copy-done.1, s32[64,2,1728]{2,1,0:T(2,128)S(1)} %copy-done, bf16[256,256]{1,0:T(8,128)(2,1)S(1)} %copy-done.9, ...), custom_call_target="tpu_custom_call" | custom-call | tf_op jit(solution)/shard_map/pallas_call | solution.py:143
  39.5 55.0 %all-gather = f32[64,1,3456]{2,1,0:T(1,128)S(1)} all-gather(f32[1,1,3456]{2,1,0:T(1,128)S(1)} %bitcast.9), channel_id=1, replica_groups=mesh['rep'=64,'fsdp'=4] {'rep'}, dimensions={0}, use_global_device_ids=true | all-gather | bytes 898560 | tf_op jit(solution)/shard_map/all_gather | solution.py:261
  94.5 0.1 copy.26
  94.6 0.0 copy-done.2
  94.6 0.0 copy-done.7
  94.6 0.0 copy-done.10
  94.6 0.0 copy-done.13
  94.6 28.6 %shard_map.176 = (f32[128,6912]{1,0:T(8,128)}, bf16[128,6912]{1,0:T(8,128)(2,1)S(1)}) custom-call(f32[64,3456]{1,0:T(8,128)S(1)} %bitcast.8, s32[64,3456]{1,0:T(8,128)S(1)} %reshape.13.index_ref, f32[128,6912]{1,0:T(8,128)S(1)} %copy-done.2, bf16[256,256]{1,0:T(8,128)(2,1)S(1)} %copy-done.6, bf16[256,256]{1,0:T(8,128)(2,1)S(1)} %copy-done.5, ...), custom_call_target="tpu_custom_call" | custom-call | tf_op jit(solution)/shard_map/pallas_call | solution.py:242
  123.2 0.0 copy-start.4
  123.2 1.2 copy-done.4
  124.4 0.0 all-gather.3.cloned.1.call-update
  124.5 72.2 %all-gather.3.cloned.1.call-done = bf16[128,27648]{1,0:T(8,128)(2,1)} async-done(((bf16[128,6912]{1,0:T(8,128)(2,1)}), bf16[128,27648]{1,0:T(8,128)(2,1)}) %all-gather.3.cloned.1.call-update) | async-done | bytes 7077904 | tf_op jit(solution)/shard_map/all_gather | solution.py:263
  196.7 6.4 %copy.28 = bf16[128,27648]{1,0:T(8,128)(2,1)} copy(bf16[128,27648]{1,0:T(8,128)(2,1)} %all-gather.3.cloned.1.call-done) | data formatting | bytes 14155776
Async XLA Ops:
  7.2 189.5 %all-gather.3.cloned.1.call-start = ((), (), s32[]{:S(2)}) async-start(), calls=%async_computation | async-start | bytes 8847360 | tf_op jit(solution)/shard_map/all_gather | solution.py:263
  10.6 7.2 %copy-start = (s32[64,2,1728]{2,1,0:T(2,128)S(1)}, s32[64,2,1728]{2,1,0:T(2,128)}, u32[]{:S(2)}) copy-start(s32[64,2,1728]{2,1,0:T(2,128)} %index_ref.1) | copy-start | bytes 2654212
  10.6 7.2 %copy-start.5 = (bf16[256,256]{1,0:T(8,128)(2,1)S(1)}, bf16[256,256]{1,0:T(8,128)(2,1)}, u32[]{:S(2)}) copy-start(bf16[256,256]{1,0:T(8,128)(2,1)} %constant.33.clone.rt_lo) | copy-start | bytes 393220
  10.6 7.2 %copy-start.6 = (bf16[256,256]{1,0:T(8,128)(2,1)S(1)}, bf16[256,256]{1,0:T(8,128)(2,1)}, u32[]{:S(2)}) copy-start(bf16[256,256]{1,0:T(8,128)(2,1)} %constant.32.clone.rt_hi) | copy-start | bytes 393220
  10.6 7.2 %copy-start.8 = (bf16[256,256]{1,0:T(8,128)(2,1)S(1)}, bf16[256,256]{1,0:T(8,128)(2,1)}, u32[]{:S(2)}) copy-start(bf16[256,256]{1,0:T(8,128)(2,1)} %constant.31.clone.r_lo) | copy-start | bytes 393220
  10.6 7.2 %copy-start.9 = (bf16[256,256]{1,0:T(8,128)(2,1)S(1)}, bf16[256,256]{1,0:T(8,128)(2,1)}, u32[]{:S(2)}) copy-start(bf16[256,256]{1,0:T(8,128)(2,1)} %constant.30.clone.r_hi) | copy-start | bytes 393220
  10.6 7.2 %copy-start.11 = (bf16[128,256]{1,0:T(8,128)(2,1)S(1)}, bf16[128,256]{1,0:T(8,128)(2,1)}, u32[]{:S(2)}) copy-start(bf16[128,256]{1,0:T(8,128)(2,1)} %constant.36.clone.lt_pair) | copy-start | bytes 196612
  10.6 7.2 %copy-start.12 = (bf16[128,256]{1,0:T(8,128)(2,1)S(1)}, bf16[128,256]{1,0:T(8,128)(2,1)}, u32[]{:S(2)}) copy-start(bf16[128,256]{1,0:T(8,128)(2,1)} %constant.34.clone.l_pair) | copy-start | bytes 196612
  10.6 7.2 %copy-start.14 = (bf16[64,256]{1,0:T(8,128)(2,1)S(1)}, bf16[64,256]{1,0:T(8,128)(2,1)}, u32[]{:S(2)}) copy-start(bf16[64,256]{1,0:T(8,128)(2,1)} %constant.38.clone.spread_ref) | copy-start | bytes 98308
  10.6 7.2 %copy-start.15 = (bf16[128,128]{1,0:T(8,128)(2,1)S(1)}, bf16[128,128]{1,0:T(8,128)(2,1)}, u32[]{:S(2)}) copy-start(bf16[128,128]{1,0:T(8,128)(2,1)} %constant.37.clone.lt_lo) | copy-start | bytes 98308
  10.6 7.2 %copy-start.16 = (bf16[128,128]{1,0:T(8,128)(2,1)S(1)}, bf16[128,128]{1,0:T(8,128)(2,1)}, u32[]{:S(2)}) copy-start(bf16[128,128]{1,0:T(8,128)(2,1)} %constant.35.clone.l_lo) | copy-start | bytes 98308
  17.9 2.0 copy-start.1
  19.9 1.5 copy-start.3
  21.3 73.2 %copy-start.2 = (f32[128,6912]{1,0:T(8,128)S(1)}, f32[128,6912]{1,0:T(8,128)}, u32[]{:S(2)}) copy-start(f32[128,6912]{1,0:T(8,128)} %master_ref.1) | copy-start | bytes 10616836
  21.3 73.2 %copy-start.7 = (bf16[256,256]{1,0:T(8,128)(2,1)S(1)}, bf16[256,256]{1,0:T(8,128)(2,1)}, u32[]{:S(2)}) copy-start(bf16[256,256]{1,0:T(8,128)(2,1)} %constant.41.clone.ones_ref) | copy-start | bytes 393220
  21.3 73.3 %copy-start.10 = (bf16[128,256]{1,0:T(8,128)(2,1)S(1)}, bf16[128,256]{1,0:T(8,128)(2,1)}, u32[]{:S(2)}) copy-start(bf16[128,256]{1,0:T(8,128)(2,1)} %constant.39.clone.b_pair) | copy-start | bytes 196612
  21.3 73.3 %copy-start.13 = (bf16[128,128]{1,0:T(8,128)(2,1)S(1)}, bf16[128,128]{1,0:T(8,128)(2,1)}, u32[]{:S(2)}) copy-start(bf16[128,128]{1,0:T(8,128)(2,1)} %constant.40.clone.b_lo) | copy-start | bytes 98308
  123.2 1.2 copy-start.4
Sparse Core Ops, SparseCore 0:
  124.6 72.0 all-gather.2
where the time goes:
time: 210 us
  waiting for transfers between devices  72.2 us (34%)
  blocking collectives  55 us (26%)
  Pallas kernels  46.8 us (22%)
  local copies, waits for them, and re-layouts  21.7 us (10%)
  between operations  14.2 us (7%)
    all_gather x1, waiting for transfers between devices, shards(): weights_full = lax.all_gather(weights_local, 'fsdp', axis=1, tiled=True)  72.2 us
    all_gather x1, blocking collectives, shards(): bands = lax.all_gather(band, 'rep', axis=0, tiled=True)  55 us
    pallas_call x1, Pallas kernels, shared_part(): pl.pallas_call(shared_kernel, grid=(steps,), in_specs=[lanes, lanes, slab...  28.6 us
    pallas_call x1, Pallas kernels, local_part(): pl.pallas_call(local_kernel, grid_spec=pltpu.PrefetchScalarGridSpec(num_s...  18.2 us
    unnamed x37, local copies, waits for them, and re-layouts  12.5 us
    transpose x1, local copies, waits for them, and re-layouts, by_group(): return split_up.transpose(0, 2, 1, 3).reshape(reps, 2 * lanes)  4.52 us
  transfers between devices with their start and end apart: 1, of which 1 were waited for; matrix products, arithmetic and copies ran while one was open for 0% of the time, Pallas kernels for 0%

commit v1 on v0

--- a/solution.py
+++ b/solution.py
@@ -19,6 +19,7 @@
 
 bf16 = jnp.bfloat16
 f32 = jnp.float32
+MESH = pl.DeviceIdType.MESH
 
 
 def dct64():
@@ -123,7 +124,7 @@
         sums = jnp.where(zmine, sums, 0.0)
         top = jnp.sum(sums[:BLOCK], axis=0, keepdims=True)
         bottom = jnp.sum(sums[BLOCK:], axis=0, keepdims=True)
-        band_ref[:, g * 128 : (g + 1) * 128] = jnp.concatenate([top, bottom], axis=1)
+        band_ref[pl.ds(step * PER_STEP + g, 1), :] = jnp.concatenate([top, bottom], axis=1)
         back = times_left(lt_pair, lt_lo, times_right(kept, rt_hi, rt_lo))
         fresh_ref[0, :, cols] = acc - back
 
@@ -147,21 +148,19 @@
             grid=(steps,),
             in_specs=[slab, slab, pl.BlockSpec((1, 2, band_index.shape[2]), lambda s, own: (own[0], 0, 0))]
             + [full(c.shape) for c in consts],
-            out_specs=[slab, pl.BlockSpec((1, PER_STEP * 128), lambda s, own: (0, s))],
+            out_specs=[slab, full((groups, 128))],
             scratch_shapes=[pltpu.VMEM((groups, 2 * BLOCK, BLOCK), bf16)],
         ),
         out_shape=[
             jax.ShapeDtypeStruct(grads.shape, f32),
-            jax.ShapeDtypeStruct((1, groups * 128), f32),
+            jax.ShapeDtypeStruct((groups, 128), f32),
         ],
         compiler_params=pltpu.CompilerParams(vmem_limit_bytes=32 * 2**20),
     )(own, grads, momentum, band_index, *[jnp.asarray(c) for c in consts])
 
 
 def summed_coefficients(band, index):
-    reps = band.shape[0]
-    band_t = band.T
-    within = index.T & 255
+    reps = band.shape[1] // 2
     half = jnp.where(lax.broadcasted_iota(jnp.int32, (8, 2 * reps), 1) >= reps, 4, 0)
     eight = lax.broadcasted_iota(jnp.int32, (8, 2 * reps), 0)
     k2_of = lax.broadcasted_iota(jnp.int32, (BLOCK, 2 * reps), 0)
@@ -171,10 +170,9 @@
     for p in range(2):
         values, codes, places = [], [], []
         for q in range(4):
-            base = p * 64 + q * 16
-            join = lambda x: jnp.concatenate([x[base : base + 8], x[base + 8 : base + 16]], axis=1)
-            w = join(within)
-            values.append(join(band_t))
+            base = (p * 4 + q) * 8
+            w = index[base : base + 8]
+            values.append(band[base : base + 8])
             codes.append((w >> 6) + half)
             places.append(w & 63)
         for t in range(4):
@@ -222,23 +220,22 @@
 
 def shared_kernel(band_ref, index_ref, master_ref, rt_hi, rt_lo, b_pair, b_lo, ones_ref, update_ref, weights_ref):
     for g in range(PER_STEP):
-        lanes = slice(g * 128, (g + 1) * 128)
+        lanes = slice(g * 64, (g + 1) * 64)
         cols = slice(g * GROUP, (g + 1) * GROUP)
         update, weights = shared_group(
-            band_ref[:, lanes], index_ref[:, lanes], master_ref[:, cols], rt_hi, rt_lo, b_pair, b_lo, ones_ref
+            band_ref[lanes, :], index_ref[lanes, :], master_ref[:, cols], rt_hi, rt_lo, b_pair, b_lo, ones_ref
         )
         update_ref[:, cols] = update
         weights_ref[:, cols] = weights
 
 
 def shared_part(bands, index, master):
-    reps = bands.shape[0]
     rows, cols = master.shape
     steps = cols // (GROUP * PER_STEP)
     t = TABLES
     consts = [*t["right_t"], *t["back"], t["ones"]]
     slab = pl.BlockSpec((rows, PER_STEP * GROUP), lambda s: (0, s))
-    lanes = pl.BlockSpec((reps, PER_STEP * 128), lambda s: (0, s))
+    lanes = pl.BlockSpec((PER_STEP * 64, 128), lambda s: (s, 0))
     return pl.pallas_call(
         shared_kernel,
         grid=(steps,),
@@ -249,17 +246,119 @@
     )(bands, index, master, *[jnp.asarray(c) for c in consts])
 
 
-def by_group(band_index):
+def rep_parts(r):
+    return r // 16, (r // 2) % 8, r % 2
+
+
+def rep_of(x, z, core):
+    return x * 16 + z * 2 + core
+
+
+def gather_kernel(
+    band_ref, index_ref, band_out, index_out, rows, index_rows,
+    own_sem, index_sem, z_send, z_recv, x_send, x_recv, s_send, s_recv,
+):
+    x, z, core = rep_parts(lax.axis_index("rep"))
+    groups = rows.shape[1]
+    other = 1 - core
+    z_peers = [rep_of(x, lax.rem(z + d, 8), core) for d in range(1, 8)]
+    x_peers = [rep_of(lax.rem(x + d, 4), z, core) for d in range(1, 4)]
+    sibling = rep_of(x, z, other)
+
+    mine = core * 32 + x * 8 + z
+    own = pltpu.make_async_copy(band_ref, rows.at[mine], own_sem)
+    own.start()
+    pulls = []
+    for c in range(2):
+        pull = pltpu.make_async_copy(index_ref.at[:, :, c], index_rows.at[c], index_sem.at[c])
+        pull.start()
+        pulls.append(pull)
+
+    barrier = pltpu.get_barrier_semaphore()
+    for peer in z_peers + x_peers + [sibling]:
+        pl.semaphore_signal(barrier, inc=1, device_id={"rep": peer}, device_id_type=MESH)
+    pl.semaphore_wait(barrier, 11)
+    own.wait()
+
+    def remote(ref, send, recv, peer):
+        return pltpu.make_async_remote_copy(
+            src_ref=ref, dst_ref=ref, send_sem=send, recv_sem=recv,
+            device_id={"rep": peer}, device_id_type=MESH,
+        )
+
+    z_copies = [remote(rows.at[mine], z_send.at[d], z_recv.at[d], peer) for d, peer in enumerate(z_peers)]
+    for copy in z_copies:
+        copy.start()
+
+    for pull in pulls:
+        pull.wait()
+    for p in range(2):
+        for k in range((groups + 1) // 2):
+            lanes = min(128, groups * BLOCK - k * 128)
+            chunk = index_rows[:, :, :, p, k * 128 : k * 128 + lanes].reshape(64, lanes)
+            turned = chunk.T & 255
+            for b in range(lanes // BAND):
+                g = 2 * k + b // 4
+                at = ((g * 2 + p) * 4 + b % 4) * 8
+                index_out[at : at + 8, :] = jnp.concatenate(
+                    [turned[b * 16 : b * 16 + 8], turned[b * 16 + 8 : b * 16 + 16]], axis=1
+                )
+
+    for copy in z_copies:
+        copy.wait()
+    bundle = rows.at[pl.ds(core * 32 + x * 8, 8)]
+    x_copies = [remote(bundle, x_send.at[d], x_recv.at[d], peer) for d, peer in enumerate(x_peers)]
+    for copy in x_copies:
+        copy.start()
+    s_copies = [remote(bundle, s_send.at[0], s_recv.at[0], sibling)]
+    s_copies[0].start()
+    for d in range(1, 4):
+        x_copies[d - 1].wait_recv()
+        source = lax.rem(x + 4 - d, 4)
+        part = rows.at[pl.ds(core * 32 + source * 8, 8)]
+        copy = remote(part, s_send.at[d], s_recv.at[d], sibling)
+        copy.start()
+        s_copies.append(copy)
+    for copy in x_copies:
+        copy.wait_send()
+    for copy in s_copies:
+        copy.wait()
+
+    @pl.loop(0, groups)
+    def _(g):
+        turned = rows[:, g, :].T
+        for b in range(8):
+            band_out[pl.ds(pl.multiple_of(g * 64 + b * 8, 8), 8), :] = jnp.concatenate(
+                [turned[b * 16 : b * 16 + 8], turned[b * 16 + 8 : b * 16 + 16]], axis=1
+            )
+
+
+def gather_part(band, band_index):
+    groups = band.shape[0]
     reps, _, lanes = band_index.shape
-    split_up = band_index.reshape(reps, 2, lanes // BLOCK, BLOCK)
-    return split_up.transpose(0, 2, 1, 3).reshape(reps, 2 * lanes)
+    dma = pltpu.SemaphoreType.DMA
+    shape = (groups * 64, 128)
+    return pl.pallas_call(
+        gather_kernel,
+        in_specs=[pl.BlockSpec(memory_space=pl.ANY)] * 2,
+        out_specs=[pl.BlockSpec(memory_space=pltpu.VMEM)] * 2,
+        out_shape=[jax.ShapeDtypeStruct(shape, f32), jax.ShapeDtypeStruct(shape, jnp.int32)],
+        scratch_shapes=[
+            pltpu.VMEM((reps, groups, 128), f32),
+            pltpu.VMEM((2, 4, 8, 2, lanes), jnp.int32),
+            dma, dma((2,)), dma((7,)), dma((7,)), dma((3,)), dma((3,)), dma((4,)), dma((4,)),
+        ],
+        compiler_params=pltpu.CompilerParams(
+            collective_id=0, has_side_effects=True, vmem_limit_bytes=32 * 2**20
+        ),
+    )(band, band_index.reshape(4, 8, 2, 2, lanes))
 
 
 def shards(grads, momentum, master, band_index):
     own = lax.axis_index("rep").astype(jnp.int32)[None]
     fresh, band = local_part(own, grads, momentum, band_index)
-    bands = lax.all_gather(band, "rep", axis=0, tiled=True)
-    update, weights_local = shared_part(bands, by_group(band_index), master)
+    bands, index = gather_part(band, band_index)
+    update, weights_local = shared_part(bands, index, master)
     weights_full = lax.all_gather(weights_local, "fsdp", axis=1, tiled=True)
     return (fresh, update, weights_full)
 

time: 210 us -> 178 us (0.85)
  blocking collectives: 55 us -> 0 us
  Pallas kernels: 46.8 us -> 72.3 us
  local copies, waits for them, and re-layouts: 21.7 us -> 18.7 us
    all_gather x1 -> x0, blocking collectives: 55 us -> none  [shards(): bands = lax.all_gather(band, 'rep', axis=0, tiled=True)]
    pallas_call x0 -> x1, Pallas kernels: none -> 26.9 us  [gather_part(): pl.pallas_call(gather_kernel, in_specs=[pl.BlockSpec(memory_space=pl.ANY)...]
    unnamed x37, local copies, waits for them, and re-layouts: 12.5 us -> 18.7 us
    reshape x2 -> x0, local copies, waits for them, and re-layouts: 4.69 us -> none  [the longest x1 2.59 us: by_group(): return split_up.transpose(0, 2, 1, 3).reshape(reps, 2 * lanes)]
    transpose x1 -> x0, local copies, waits for them, and re-layouts: 4.52 us -> none  [by_group(): return split_up.transpose(0, 2, 1, 3).reshape(reps, 2 * lanes)]
where the time goes in v1:
time: 178 us
  waiting for transfers between devices  72.6 us (41%)
  Pallas kernels  72.3 us (41%)
  local copies, waits for them, and re-layouts  18.7 us (11%)
  between operations  14.1 us (8%)
    all_gather x1, waiting for transfers between devices, shards(): weights_full = lax.all_gather(weights_local, 'fsdp', axis=1, tiled=True)  72.6 us
    pallas_call x1, Pallas kernels, shared_part(): pl.pallas_call(shared_kernel, grid=(steps,), in_specs=[lanes, lanes, slab...  27.1 us
    pallas_call x1, Pallas kernels, gather_part(): pl.pallas_call(gather_kernel, in_specs=[pl.BlockSpec(memory_space=pl.ANY)...  26.9 us
    unnamed x37, local copies, waits for them, and re-layouts  18.7 us
    pallas_call x1, Pallas kernels, local_part(): pl.pallas_call(local_kernel, grid_spec=pltpu.PrefetchScalarGridSpec(num_s...  18.3 us
  transfers between devices with their start and end apart: 1, of which 1 were waited for; matrix products, arithmetic and copies ran while one was open for 0% of the time, Pallas kernels for 0%

profile of v1, /device:TPU:1, one launch (start us, length us, event | category | flops | bytes accessed | tf_op | source)
XLA Modules:
  0.0 177.7 jit_solution(5382517970866769377)
XLA Ops:
  7.2 0.0 all-gather.2.cloned.1.call-start
  7.2 0.0 copy-start
  7.2 1.2 copy-done
  8.4 0.0 copy-start.1
  8.4 2.0 %copy-done.1 = f32[1,128,6912]{2,1,0:T(8,128)S(1)} copy-done((f32[1,128,6912]{2,1,0:T(8,128)S(1)}, f32[1,128,6912]{2,1,0:T(8,128)}, u32[]{:S(2)}) %copy-start.1) | copy-done | bytes 3538968
  10.4 0.0 copy-start.3
  10.4 1.5 copy-done.3
  11.9 0.0 copy-start.4
  11.9 0.9 copy-done.4
  12.8 0.0 copy-start.6
  12.8 0.9 copy-done.6
  13.7 0.0 copy-start.9
  13.7 0.9 copy-done.9
  14.6 0.0 copy-start.10
  14.6 0.9 copy-done.10
  15.5 0.0 copy-start.12
  15.5 0.8 copy-done.12
  16.3 0.0 copy-start.13
  16.3 0.8 copy-done.13
  17.2 0.0 copy-start.15
  17.2 0.8 copy-done.15
  17.9 0.0 copy-start.16
  17.9 0.8 copy-done.16
  18.7 0.0 copy-start.17
  18.7 0.8 copy-done.17
  19.4 0.0 copy-start.2
  19.4 0.0 copy-start.5
  19.5 0.0 copy-start.7
  19.5 0.0 copy-start.8
  19.5 0.0 copy-start.11
  19.5 0.0 copy-start.14
  19.5 18.3 %shard_map.175 = (f32[1,128,6912]{2,1,0:T(8,128)}, f32[27,128]{1,0:T(8,128)S(1)}) custom-call(s32[1]{0:T(128)} %bitcast.own_ref, bf16[1,128,6912]{2,1,0:T(8,128)(2,1)S(1)} %copy-done.3, f32[1,128,6912]{2,1,0:T(8,128)S(1)} %copy-done.1, s32[64,2,1728]{2,1,0:T(2,128)S(1)} %copy-done, bf16[256,256]{1,0:T(8,128)(2,1)S(1)} %copy-done.10, ...), custom_call_target="tpu_custom_call" | custom-call | tf_op jit(solution)/shard_map/pallas_call | solution.py:144
  37.8 26.9 %shard_map.176 = (f32[1728,128]{1,0:T(8,128)S(1)}, s32[1728,128]{1,0:T(8,128)S(1)}) custom-call(f32[27,128]{1,0:T(8,128)S(1)} %get-tuple-element.10.band_ref, s32[4,8,2,2,1728]{4,3,2,1,0:T(2,128)S(1)} %bitcast.2), custom_call_target="tpu_custom_call" | custom-call | tf_op jit(solution)/shard_map/pallas_call | solution.py:341
  64.7 0.0 copy-done.2
  64.7 0.0 copy-done.5
  64.7 0.0 copy-done.7
  64.7 0.0 copy-done.8
  64.7 0.0 copy-done.11
  64.8 0.0 copy-done.14
  64.8 27.1 %shard_map.177 = (f32[128,6912]{1,0:T(8,128)}, bf16[128,6912]{1,0:T(8,128)(2,1)}) custom-call(f32[1728,128]{1,0:T(8,128)S(1)} %get-tuple-element.11.band_ref, s32[1728,128]{1,0:T(8,128)S(1)} %get-tuple-element.12.index_ref, f32[128,6912]{1,0:T(8,128)S(1)} %copy-done.2, bf16[256,256]{1,0:T(8,128)(2,1)S(1)} %copy-done.7, bf16[256,256]{1,0:T(8,128)(2,1)S(1)} %copy-done.5, ...), custom_call_target="tpu_custom_call" | custom-call | tf_op jit(solution)/shard_map/pallas_call | solution.py:239
  91.8 0.0 all-gather.2.cloned.1.call-update
  91.8 72.6 %all-gather.2.cloned.1.call-done = bf16[128,27648]{1,0:T(8,128)(2,1)} async-done(((bf16[128,6912]{1,0:T(8,128)(2,1)}), bf16[128,27648]{1,0:T(8,128)(2,1)}) %all-gather.2.cloned.1.call-update) | async-done | bytes 7077904 | tf_op jit(solution)/shard_map/all_gather | solution.py:362
  164.4 6.4 %copy.20 = bf16[128,27648]{1,0:T(8,128)(2,1)} copy(bf16[128,27648]{1,0:T(8,128)(2,1)} %all-gather.2.cloned.1.call-done) | data formatting | bytes 14155776
Async XLA Ops:
  7.2 157.3 %all-gather.2.cloned.1.call-start = ((), (), s32[]{:S(2)}) async-start(), calls=%async_computation | async-start | bytes 8847360 | tf_op jit(solution)/shard_map/all_gather | solution.py:362
  7.2 1.2 copy-start
  8.4 2.0 %copy-start.1 = (f32[1,128,6912]{2,1,0:T(8,128)S(1)}, f32[1,128,6912]{2,1,0:T(8,128)}, u32[]{:S(2)}) copy-start(f32[1,128,6912]{2,1,0:T(8,128)} %mom_ref.1) | copy-start | bytes 10616836
  10.4 1.5 copy-start.3
  11.9 0.9 copy-start.4
  12.8 0.9 copy-start.6
  13.7 0.9 copy-start.9
  14.6 0.9 copy-start.10
  15.5 0.8 copy-start.12
  16.3 0.8 copy-start.13
  17.2 0.8 copy-start.15
  17.9 0.8 copy-start.16
  18.7 0.8 copy-start.17
  19.4 45.3 %copy-start.2 = (f32[128,6912]{1,0:T(8,128)S(1)}, f32[128,6912]{1,0:T(8,128)}, u32[]{:S(2)}) copy-start(f32[128,6912]{1,0:T(8,128)} %master_ref.1) | copy-start | bytes 10616836
  19.4 45.3 %copy-start.5 = (bf16[256,256]{1,0:T(8,128)(2,1)S(1)}, bf16[256,256]{1,0:T(8,128)(2,1)}, u32[]{:S(2)}) copy-start(bf16[256,256]{1,0:T(8,128)(2,1)} %constant.33.clone.rt_lo) | copy-start | bytes 393220
  19.5 45.3 %copy-start.7 = (bf16[256,256]{1,0:T(8,128)(2,1)S(1)}, bf16[256,256]{1,0:T(8,128)(2,1)}, u32[]{:S(2)}) copy-start(bf16[256,256]{1,0:T(8,128)(2,1)} %constant.32.clone.rt_hi) | copy-start | bytes 393220
  19.5 45.3 %copy-start.8 = (bf16[256,256]{1,0:T(8,128)(2,1)S(1)}, bf16[256,256]{1,0:T(8,128)(2,1)}, u32[]{:S(2)}) copy-start(bf16[256,256]{1,0:T(8,128)(2,1)} %constant.41.clone.ones_ref) | copy-start | bytes 393220
  19.5 45.3 %copy-start.11 = (bf16[128,256]{1,0:T(8,128)(2,1)S(1)}, bf16[128,256]{1,0:T(8,128)(2,1)}, u32[]{:S(2)}) copy-start(bf16[128,256]{1,0:T(8,128)(2,1)} %constant.39.clone.b_pair) | copy-start | bytes 196612
  19.5 45.3 %copy-start.14 = (bf16[128,128]{1,0:T(8,128)(2,1)S(1)}, bf16[128,128]{1,0:T(8,128)(2,1)}, u32[]{:S(2)}) copy-start(bf16[128,128]{1,0:T(8,128)(2,1)} %constant.40.clone.b_lo) | copy-start | bytes 98308
Sparse Core Ops, SparseCore 0:
  92.0 72.4 all-gather.1

commit v2 on v1

--- a/solution.py
+++ b/solution.py
@@ -20,6 +20,7 @@
 bf16 = jnp.bfloat16
 f32 = jnp.float32
 MESH = pl.DeviceIdType.MESH
+VMEM_LIMIT = 60 * 2**20
 
 
 def dct64():
@@ -88,10 +89,12 @@
 
 
 def local_kernel(
-    own_ref, grads_ref, mom_ref, index_ref,
-    r_hi, r_lo, rt_hi, rt_lo, l_pair, l_lo, lt_pair, lt_lo, spread_ref,
-    fresh_ref, band_ref, wide,
+    own_ref, grads_ref, mom_ref, index_ref, table_ref, fresh_ref, band_ref, wide,
 ):
+    r_hi, r_lo, rt_hi, rt_lo = (table_ref.at[k * 256 : (k + 1) * 256] for k in range(4))
+    l_pair, lt_pair = (table_ref.at[1024 + k * 128 : 1152 + k * 128] for k in range(2))
+    l_lo, lt_lo = (table_ref.at[1280:1408, k * 128 : (k + 1) * 128] for k in range(2))
+    spread_ref = table_ref.at[1408:1472]
     step = pl.program_id(0)
     groups = wide.shape[0]
 
@@ -139,7 +142,10 @@
     steps = groups // PER_STEP
     width = PER_STEP * GROUP
     t = TABLES
-    consts = [*t["right"], *t["right_t"], *t["left"], *t["left_t"], t["spread"]]
+    lows = np.concatenate([t["left"][1], t["left_t"][1]], axis=1)
+    table = np.concatenate(
+        [*t["right"], *t["right_t"], t["left"][0], t["left_t"][0], lows, t["spread"]], axis=0
+    )
     slab = pl.BlockSpec((1, 2 * BLOCK, width), lambda s, own: (0, 0, s))
     return pl.pallas_call(
         local_kernel,
@@ -147,7 +153,7 @@
             num_scalar_prefetch=1,
             grid=(steps,),
             in_specs=[slab, slab, pl.BlockSpec((1, 2, band_index.shape[2]), lambda s, own: (own[0], 0, 0))]
-            + [full(c.shape) for c in consts],
+            + [full(table.shape)],
             out_specs=[slab, full((groups, 128))],
             scratch_shapes=[pltpu.VMEM((groups, 2 * BLOCK, BLOCK), bf16)],
         ),
@@ -155,8 +161,8 @@
             jax.ShapeDtypeStruct(grads.shape, f32),
             jax.ShapeDtypeStruct((groups, 128), f32),
         ],
-        compiler_params=pltpu.CompilerParams(vmem_limit_bytes=32 * 2**20),
-    )(own, grads, momentum, band_index, *[jnp.asarray(c) for c in consts])
+        compiler_params=pltpu.CompilerParams(vmem_limit_bytes=VMEM_LIMIT),
+    )(own, grads, momentum, band_index, jnp.asarray(table))
 
 
 def summed_coefficients(band, index):
@@ -218,32 +224,15 @@
     return update, (master - learn_rate * update).astype(bf16)
 
 
-def shared_kernel(band_ref, index_ref, master_ref, rt_hi, rt_lo, b_pair, b_lo, ones_ref, update_ref, weights_ref):
-    for g in range(PER_STEP):
-        lanes = slice(g * 64, (g + 1) * 64)
-        cols = slice(g * GROUP, (g + 1) * GROUP)
-        update, weights = shared_group(
-            band_ref[lanes, :], index_ref[lanes, :], master_ref[:, cols], rt_hi, rt_lo, b_pair, b_lo, ones_ref
-        )
-        update_ref[:, cols] = update
-        weights_ref[:, cols] = weights
-
-
-def shared_part(bands, index, master):
-    rows, cols = master.shape
-    steps = cols // (GROUP * PER_STEP)
+def shared_table_array():
     t = TABLES
-    consts = [*t["right_t"], *t["back"], t["ones"]]
-    slab = pl.BlockSpec((rows, PER_STEP * GROUP), lambda s: (0, s))
-    lanes = pl.BlockSpec((PER_STEP * 64, 128), lambda s: (s, 0))
-    return pl.pallas_call(
-        shared_kernel,
-        grid=(steps,),
-        in_specs=[lanes, lanes, slab] + [full(c.shape) for c in consts],
-        out_specs=[slab, slab],
-        out_shape=[jax.ShapeDtypeStruct(master.shape, f32), jax.ShapeDtypeStruct(master.shape, bf16)],
-        compiler_params=pltpu.CompilerParams(vmem_limit_bytes=32 * 2**20),
-    )(bands, index, master, *[jnp.asarray(c) for c in consts])
+    pair, low = t["back"]
+    low = np.concatenate([low, np.zeros_like(low)], axis=1)
+    return jnp.asarray(np.concatenate([*t["right_t"], t["ones"], pair, low], axis=0))
+
+
+def shared_tables(ref):
+    return ref.at[0:256], ref.at[256:512], ref.at[768:896], ref.at[896:1024, 0:128], ref.at[512:768]
 
 
 def rep_parts(r):
@@ -349,17 +338,213 @@
             dma, dma((2,)), dma((7,)), dma((7,)), dma((3,)), dma((3,)), dma((4,)), dma((4,)),
         ],
         compiler_params=pltpu.CompilerParams(
-            collective_id=0, has_side_effects=True, vmem_limit_bytes=32 * 2**20
+            collective_id=0, has_side_effects=True, vmem_limit_bytes=VMEM_LIMIT
         ),
     )(band, band_index.reshape(4, 8, 2, 2, lanes))
+
+
+UNITS = 7
+WIDE = 2 * GROUP
+DIRECT = 64
+
+
+def update_kernel(
+    band_ref, index_ref, master_ref, table_ref, update_out, weights_out,
+    masters, updates, slots,
+    m_sem, y_send, y_recv, x_send, x_recv, s_send, s_recv, o_sem, t_sem,
+):
+    rep = lax.axis_index("rep")
+    shard = lax.axis_index("fsdp")
+    x, z, core = rep_parts(rep)
+    cols = masters.shape[1]
+    groups = cols // GROUP
+    sibling = rep_of(x, z, 1 - core)
+    y_peers = [lax.rem(shard + d, 4) for d in range(1, 4)]
+    x_peers = [rep_of(lax.rem(x + d, 4), z, core) for d in range(1, 4)]
+    share = (2 * BLOCK - DIRECT) // 4
+
+    def first_group(of_core, unit):
+        return 2 * unit + of_core * (groups - 2 - 4 * unit)
+
+    def span(of_core, unit):
+        return pl.ds(pl.multiple_of(first_group(of_core, unit) * GROUP, GROUP), WIDE)
+
+    def last_span(of_core):
+        start = (groups // 2 - 1 + 2 * of_core) * GROUP
+        return pl.ds(pl.multiple_of(start, GROUP), GROUP)
+
+    def master_copy(unit):
+        at = span(core, unit)
+        return pltpu.make_async_copy(master_ref.at[:, at], masters.at[:, at], m_sem.at[unit])
+
+    def share_rows(of_x):
+        return pl.ds(pl.multiple_of(DIRECT + of_x * share, 16), share)
+
+    def y_copies(unit):
+        at = span(core, unit)
+        out = []
+        for d in range(3):
+            for k, rows in enumerate((pl.ds(0, DIRECT), share_rows(x))):
+                out.append(pltpu.make_async_remote_copy(
+                    src_ref=slots.at[0, rows, at], dst_ref=slots.at[d + 1, rows, at],
+                    send_sem=y_send.at[unit, d, k], recv_sem=y_recv.at[unit, d, k],
+                    device_id={"fsdp": y_peers[d]}, device_id_type=MESH,
+                ))
+        return out
+
+    def x_copies(unit, arriving):
+        at = span(core, unit)
+        out = []
+        for d in range(3):
+            rows = share_rows(lax.rem(x + 3 - d, 4) if arriving else x)
+            part = slots.at[pl.ds(1, 3), rows, at]
+            out.append(pltpu.make_async_remote_copy(
+                src_ref=part, dst_ref=part, send_sem=x_send.at[unit, d], recv_sem=x_recv.at[unit, d],
+                device_id={"rep": x_peers[d]}, device_id_type=MESH,
+            ))
+        return out
+
+    def s_copies(unit, at):
+        return [
+            pltpu.make_async_remote_copy(
+                src_ref=part, dst_ref=part, send_sem=s_send.at[unit, k], recv_sem=s_recv.at[unit, k],
+                device_id={"rep": sibling}, device_id_type=MESH,
+            )
+            for k, part in enumerate((slots.at[:, :, at], updates.at[:, at]))
+        ]
+
+    def out_copies(sems, unit, at):
+        out = [pltpu.make_async_copy(updates.at[:, at], update_out.at[:, at], sems.at[unit, 4])]
+        for d in range(4):
+            from_shard = lax.rem(shard + 4 - d, 4)
+            place = pl.ds(pl.multiple_of(from_shard * cols + at.start, GROUP), at.size)
+            out.append(pltpu.make_async_copy(slots.at[d, :, at], weights_out.at[:, place], sems.at[unit, d]))
+        return out
+
+    def by_width(of_core, unit, act):
+        @pl.when(unit < UNITS - 1)
+        def _():
+            act(span(of_core, unit))
+
+        @pl.when(unit == UNITS - 1)
+        def _():
+            act(last_span(of_core))
+
+    @pl.loop(0, UNITS)
+    def _(unit):
+        master_copy(unit).start()
+
+    barrier = pltpu.get_barrier_semaphore()
+    for peer in y_peers:
+        pl.semaphore_signal(barrier, inc=1, device_id={"fsdp": peer}, device_id_type=MESH)
+    for peer in x_peers + [sibling]:
+        pl.semaphore_signal(barrier, inc=1, device_id={"rep": peer}, device_id_type=MESH)
+    pl.semaphore_wait(barrier, 7)
+
+    tables = shared_tables(table_ref)
+
+    @pl.loop(0, UNITS + 3)
+    def _(step):
+        @pl.when(step < UNITS)
+        def _():
+            master_copy(step).wait()
+
+            @pl.loop(0, 2)
+            def _(k):
+                g = first_group(core, step) + k
+                lanes = pl.ds(pl.multiple_of(g * 64, 64), 64)
+                at = pl.ds(pl.multiple_of(g * GROUP, GROUP), GROUP)
+                update, weights = shared_group(band_ref[lanes, :], index_ref[lanes, :], masters[:, at], *tables)
+                updates[:, at] = update
+                slots[0, :, at] = weights
+
+            for copy in y_copies(step):
+                copy.start()
+
+        @pl.when((step >= 1) & (step < UNITS + 1))
+        def _():
+            for copy in y_copies(step - 1):
+                copy.wait_recv()
+            for copy in x_copies(step - 1, False):
+                copy.start()
+
+        @pl.when((step >= 2) & (step < UNITS + 2))
+        def _():
+            unit = step - 2
+            for copy in x_copies(unit, True):
+                copy.wait_recv()
+
+            def act(at):
+                for copy in s_copies(unit, at):
+                    copy.start()
+
+            by_width(core, unit, act)
+            for copy in out_copies(o_sem, unit, span(core, unit)):
+                copy.start()
+
+        @pl.when(step >= 3)
+        def _():
+            unit = step - 3
+
+            def act(at):
+                for copy in s_copies(unit, at):
+                    copy.wait_recv()
+                for copy in out_copies(t_sem, unit, at):
+                    copy.start()
+
+            by_width(1 - core, unit, act)
+
+    @pl.loop(0, UNITS)
+    def _(unit):
+        for copy in y_copies(unit) + x_copies(unit, False):
+            copy.wait_send()
+        for copy in out_copies(o_sem, unit, span(core, unit)):
+            copy.wait()
+
+        def drain_own(at):
+            for copy in s_copies(unit, at):
+                copy.wait_send()
+
+        def drain_other(at):
+            for copy in out_copies(t_sem, unit, at):
+                copy.wait()
+
+        by_width(core, unit, drain_own)
+        by_width(1 - core, unit, drain_other)
+
+
+def update_part(bands, index, master):
+    rows, cols = master.shape
+    dma = pltpu.SemaphoreType.DMA
+    table = shared_table_array()
+    vmem = pl.BlockSpec(memory_space=pltpu.VMEM)
+    anywhere = pl.BlockSpec(memory_space=pl.ANY)
+    return pl.pallas_call(
+        update_kernel,
+        in_specs=[vmem, vmem, anywhere, vmem],
+        out_specs=[anywhere, anywhere],
+        out_shape=[
+            jax.ShapeDtypeStruct(master.shape, f32),
+            jax.ShapeDtypeStruct((rows, 4 * cols), bf16),
+        ],
+        scratch_shapes=[
+            pltpu.VMEM((rows, cols), f32),
+            pltpu.VMEM((rows, cols), f32),
+            pltpu.VMEM((4, rows, cols), bf16),
+            dma((UNITS,)), dma((UNITS, 3, 2)), dma((UNITS, 3, 2)), dma((UNITS, 3)), dma((UNITS, 3)),
+            dma((UNITS, 2)), dma((UNITS, 2)), dma((UNITS, 5)), dma((UNITS, 5)),
+        ],
+        compiler_params=pltpu.CompilerParams(
+            collective_id=1, has_side_effects=True, vmem_limit_bytes=VMEM_LIMIT
+        ),
+    )(bands, index, master, table)
 
 
 def shards(grads, momentum, master, band_index):
     own = lax.axis_index("rep").astype(jnp.int32)[None]
     fresh, band = local_part(own, grads, momentum, band_index)
     bands, index = gather_part(band, band_index)
-    update, weights_local = shared_part(bands, index, master)
-    weights_full = lax.all_gather(weights_local, "fsdp", axis=1, tiled=True)
+    update, weights_full = update_part(bands, index, master)
     return (fresh, update, weights_full)
 
 

time: 178 us -> 102 us (0.57)
  waiting for transfers between devices: 72.6 us -> 0 us
  Pallas kernels: 72.3 us -> 92.9 us
  between operations: 14.1 us -> 0.66 us
  local copies, waits for them, and re-layouts: 18.7 us -> 8.3 us
    all_gather x1 -> x0, waiting for transfers between devices: 72.6 us -> none  [shards(): weights_full = lax.all_gather(weights_local, 'fsdp', axis=1, tiled=True)]
    pallas_call x1, Pallas kernels: 27.1 us -> 45.7 us  [update_part(): pl.pallas_call(update_kernel, in_specs=[vmem, vmem, anywhere, vmem], out_...]
    unnamed x37 -> x4, local copies, waits for them, and re-layouts: 18.7 us -> 8.3 us
  transfers between devices with their start and end apart: 1 -> 0, of which waited for: 1 -> 0; matrix products, arithmetic and copies ran while one was open for 0% -> 0% of each run, Pallas kernels for 0% -> 0%
where the time goes in v2:
time: 102 us
  Pallas kernels  92.9 us (91%)
  local copies, waits for them, and re-layouts  8.3 us (8%)
    pallas_call x1, Pallas kernels, update_part(): pl.pallas_call(update_kernel, in_specs=[vmem, vmem, anywhere, vmem], out_...  45.7 us
    pallas_call x1, Pallas kernels, gather_part(): pl.pallas_call(gather_kernel, in_specs=[pl.BlockSpec(memory_space=pl.ANY)...  27.9 us
    pallas_call x1, Pallas kernels, local_part(): pl.pallas_call(local_kernel, grid_spec=pltpu.PrefetchScalarGridSpec(num_s...  19.3 us
    unnamed x4, local copies, waits for them, and re-layouts  8.3 us

profile of v2, /device:TPU:1, one launch (start us, length us, event | category | flops | bytes accessed | tf_op | source)
XLA Modules:
  0.0 101.9 jit_solution(17442203019540487049)
XLA Ops:
  0.6 19.3 %shard_map.85 = (f32[1,128,6912]{2,1,0:T(8,128)}, f32[27,128]{1,0:T(8,128)}) custom-call(s32[1]{0:T(128)} %bitcast.own_ref, bf16[1,128,6912]{2,1,0:T(8,128)(2,1)} %grads_ref.1, f32[1,128,6912]{2,1,0:T(8,128)} %mom_ref.1, s32[64,2,1728]{2,1,0:T(2,128)} %index_ref.1, bf16[1472,256]{1,0:T(8,128)(2,1)} %constant.10.clone.table_ref), custom_call_target="tpu_custom_call" | custom-call | tf_op jit(solution)/shard_map/pallas_call | solution.py:150
  19.9 27.9 %shard_map.86 = (f32[1728,128]{1,0:T(8,128)}, s32[1728,128]{1,0:T(8,128)}) custom-call(f32[27,128]{1,0:T(8,128)} %get-tuple-element.10.band_ref, s32[4,8,2,2,1728]{4,3,2,1,0:T(2,128)} %bitcast.2), custom_call_target="tpu_custom_call" | custom-call | tf_op jit(solution)/shard_map/pallas_call | solution.py:330
  47.8 45.7 %shard_map.87 = (f32[128,6912]{1,0:T(8,128)}, bf16[128,27648]{1,0:T(8,128)(2,1)}) custom-call(f32[1728,128]{1,0:T(8,128)} %get-tuple-element.11.band_ref, s32[1728,128]{1,0:T(8,128)} %get-tuple-element.12.index_ref, f32[128,6912]{1,0:T(8,128)} %master_ref.1, bf16[1024,256]{1,0:T(8,128)(2,1)} %constant.11.clone.table_ref), custom_call_target="tpu_custom_call" | custom-call | tf_op jit(solution)/shard_map/pallas_call | solution.py:522
  93.6 0.0 copy-start
  93.6 4.2 %copy.11 = f32[128,6912]{1,0:T(8,128)} copy(f32[128,6912]{1,0:T(8,128)} %get-tuple-element.19) | data formatting | bytes 7077888
  97.7 1.2 %copy-done = bf16[128,27648]{1,0:T(8,128)(2,1)S(1)} copy-done((bf16[128,27648]{1,0:T(8,128)(2,1)S(1)}, bf16[128,27648]{1,0:T(8,128)(2,1)}, u32[]{:S(2)}) %copy-start) | copy-done | bytes 7077912
  98.9 3.0 %copy.12 = bf16[128,27648]{1,0:T(8,128)(2,1)} copy(bf16[128,27648]{1,0:T(8,128)(2,1)S(1)} %copy-done) | data formatting | bytes 14155776
Async XLA Ops:
  93.6 5.4 %copy-start = (bf16[128,27648]{1,0:T(8,128)(2,1)S(1)}, bf16[128,27648]{1,0:T(8,128)(2,1)}, u32[]{:S(2)}) copy-start(bf16[128,27648]{1,0:T(8,128)(2,1)} %get-tuple-element.20) | copy-start | bytes 21233668

commit v3 on v0

v3 whole, which is shorter than its diff:
```python
import jax
import jax.numpy as jnp
import numpy as np
import ml_dtypes
from jax import lax
from jax.experimental import pallas as pl
from jax.experimental.pallas import tpu as pltpu
from jax.sharding import PartitionSpec as P

BLOCK = 64
BAND = 16
GROUP = 256
PER_STEP = 3

momentum_decay = 0.9
learn_rate = 0.05

bf16 = jnp.bfloat16
f32 = jnp.float32
MESH = pl.DeviceIdType.MESH
VMEM_LIMIT = 60 * 2**20


def dct64():
    k = np.arange(BLOCK, dtype=np.float64)[:, None]
    n = np.arange(BLOCK, dtype=np.float64)[None, :]
    basis = np.cos(np.pi * (2.0 * n + 1.0) * k / (2.0 * BLOCK))
    return basis * np.where(k == 0.0, np.sqrt(1.0 / BLOCK), np.sqrt(2.0 / BLOCK))


def halves(table):
    hi = table.astype(np.float32).astype(ml_dtypes.bfloat16)
    lo = (table - hi.astype(np.float64)).astype(np.float32).astype(ml_dtypes.bfloat16)
    return hi, lo


def left_pair(table):
    hi, lo = halves(table)
    return np.concatenate([hi, hi], axis=1), lo


def make_tables():
    c = dct64()
    right = np.kron(np.eye(4), c.T)
    left = np.kron(np.eye(2), c)
    m, i = np.divmod(np.arange(BLOCK), 8)
    k1 = 4 * (m + 8 * (i // 4)) + i % 4
    back_perm = np.kron(np.eye(2), c[k1].T)
    spread = np.kron(np.eye(4), np.ones((BAND, BLOCK)))
    ones = np.kron(np.eye(4), np.ones((BLOCK, BLOCK)))
    as_bf16 = lambda a: a.astype(ml_dtypes.bfloat16)
    return dict(
        right=halves(right),
        right_t=halves(right.T),
        left=left_pair(left),
        left_t=left_pair(left.T),
        back=left_pair(back_perm),
        spread=as_bf16(spread),
        ones=as_bf16(ones),
    )


TABLES = make_tables()


def split(x):
    hi = x.astype(bf16)
    return hi, (x - hi.astype(f32)).astype(bf16)


def dot(a, b):
    return jnp.dot(a, b, preferred_element_type=f32)


def dot_nt(a, b):
    return lax.dot_general(a, b, (((1,), (1,)), ((), ())), preferred_element_type=f32)


def times_right(x, hi_ref, lo_ref):
    hi, lo = split(x)
    return dot(hi, hi_ref[...]) + (dot(lo, hi_ref[...]) + dot(hi, lo_ref[...]))


def times_left(pair_ref, lo_ref, x):
    hi, lo = split(x)
    return dot(pair_ref[...], jnp.concatenate([hi, lo], axis=0)) + dot(lo_ref[...], hi)


def summed_coefficients(band, index):
    reps = band.shape[1] // 2
    half = jnp.where(lax.broadcasted_iota(jnp.int32, (8, 2 * reps), 1) >= reps, 4, 0)
    eight = lax.broadcasted_iota(jnp.int32, (8, 2 * reps), 0)
    k2_of = lax.broadcasted_iota(jnp.int32, (BLOCK, 2 * reps), 0)
    zero = jnp.zeros((8, 2 * reps), f32)
    quarter = lax.broadcasted_iota(jnp.int32, (16, GROUP), 1) >> 6
    parts = []
    for p in range(2):
        values, codes, places = [], [], []
        for q in range(4):
            base = (p * 4 + q) * 8
            w = index[base : base + 8]
            values.append(band[base : base + 8])
            codes.append((w >> 6) + half)
            places.append(w & 63)
        for t in range(4):
            his, los, hots = [], [], []
            for q in range(4):
                a, b = [], []
                for m in (2 * t, 2 * t + 1):
                    spread = lambda x: jnp.broadcast_to(x[m : m + 1], eight.shape)
                    a.append(jnp.where(spread(codes[q]) == eight, spread(values[q]), 0.0))
                    here = jnp.broadcast_to(places[q][m : m + 1], k2_of.shape) == k2_of
                    b.append(jnp.where(here, 1.0, 0.0).astype(bf16))
                left = jnp.concatenate(
                    [jnp.concatenate([a[0], zero], axis=1), jnp.concatenate([zero, a[1]], axis=1)], axis=0
                )
                hi, lo = split(left)
                his.append(hi)
                los.append(lo)
                hots.append(jnp.concatenate(b, axis=1))
            out = dot_nt(jnp.concatenate(his + los, axis=0), jnp.concatenate(hots, axis=0))
            out = out[:64] + out[64:]
            rows = jnp.where(quarter == 0, out[:16], 0.0)
            for q in range(1, 4):
                rows = jnp.where(quarter == q, out[16 * q : 16 * (q + 1)], rows)
            parts.append(rows)
    return jnp.concatenate(parts, axis=0)


def shared_group(band, index, master, rt_hi, rt_lo, b_pair, b_lo, ones_ref):
    total = summed_coefficients(band, index)
    direction = times_left(b_pair, b_lo, times_right(total, rt_hi, rt_lo))
    square = direction * direction
    sums = [
        jnp.broadcast_to(jnp.sum(square[p * BLOCK : (p + 1) * BLOCK], axis=0, keepdims=True), (8, GROUP))
        for p in range(2)
    ]
    hi, lo = split(jnp.concatenate(sums, axis=0))
    means = (dot(hi, ones_ref[...]) + dot(lo, ones_ref[...])) * (1.0 / (BLOCK * BLOCK))
    scale = 0.1 * jnp.sqrt(means + 1e-06)
    scale = jnp.concatenate(
        [jnp.broadcast_to(scale[8 * p : 8 * p + 1], (BLOCK, GROUP)) for p in range(2)], axis=0
    )
    update = direction / (jnp.abs(direction) + scale)
    return update, (master - learn_rate * update).astype(bf16)


def rep_parts(r):
    return r // 16, (r // 2) % 8, r % 2


def rep_of(x, z, core):
    return x * 16 + z * 2 + core


UNITS = 7
WIDE = 2 * GROUP
STEPS = 9
EARLY, MIDDLE = 2, 6


def kernel(
    grads_ref, mom_ref, index_ref, master_ref, table_ref,
    fresh_out, update_out, weights_out,
    grads, acc, kept_rows, wide, own_index, index_rows, places, rows, masters, updates, slots, table,
    in_sem, index_sem, f_sem, gz_send, gz_recv, gx_send, gx_recv, gs_send, gs_recv,
    m_sem, y_send, y_recv, x_send, x_recv, z_send, z_recv, s_send, s_recv, o_sem, t_sem,
):
    rep = lax.axis_index("rep")
    shard = lax.axis_index("fsdp")
    x, z, core = rep_parts(rep)
    cols = masters.shape[1]
    groups = cols // GROUP
    sibling = rep_of(x, z, 1 - core)
    y_peers = [lax.rem(shard + d, 4) for d in range(1, 4)]
    x_peers = [rep_of(lax.rem(x + d, 4), z, core) for d in range(1, 4)]
    z_peers = [rep_of(x, lax.rem(z + d, 8), core) for d in range(1, 8)]
    chunk = PER_STEP * GROUP
    tall = PER_STEP * 2 * BLOCK

    def remote(src, dst, send, recv, peer):
        return pltpu.make_async_remote_copy(
            src_ref=src, dst_ref=dst, send_sem=send, recv_sem=recv, device_id=peer, device_id_type=MESH,
        )


    def columns(step):
        return pl.ds(pl.multiple_of(step * chunk, chunk), chunk)

    def in_copies(step):
        at = columns(step)
        return (
            pltpu.make_async_copy(grads_ref.at[0, :, at], grads.at[:, at], in_sem.at[step, 0]),
            pltpu.make_async_copy(mom_ref.at[0, :, at], acc.at[:, at], in_sem.at[step, 1]),
        )

    def fresh_copy(step):
        at = columns(step)
        return pltpu.make_async_copy(acc.at[:, at], fresh_out.at[0, :, at], f_sem.at[step])

    def first_group(of_core, unit):
        return 2 * unit + of_core * (groups - 2 - 4 * unit)

    def span(of_core, unit):
        return pl.ds(pl.multiple_of(first_group(of_core, unit) * GROUP, GROUP), WIDE)

    def last_span(of_core):
        return pl.ds(pl.multiple_of((groups // 2 - 1 + 2 * of_core) * GROUP, GROUP), GROUP)

    def master_copy(unit):
        at = span(core, unit)
        return pltpu.make_async_copy(master_ref.at[:, at], masters.at[:, at], m_sem.at[unit])

    pull_own = pltpu.make_async_copy(index_ref.at[x, z, core], own_index, index_sem.at[2])
    pull_table = pltpu.make_async_copy(table_ref, table, index_sem.at[3])
    pulls = [pltpu.make_async_copy(index_ref.at[:, :, c], index_rows.at[c], index_sem.at[c]) for c in range(2)]
    pull_own.start()
    pull_table.start()

    @pl.loop(0, STEPS)
    def _(step):
        for copy in in_copies(step):
            copy.start()

    for pull in pulls:
        pull.start()

    @pl.loop(0, UNITS)
    def _(unit):
        master_copy(unit).start()

    barrier = pltpu.get_barrier_semaphore()
    for peer in y_peers:
        pl.semaphore_signal(barrier, inc=1, device_id={"fsdp": peer}, device_id_type=MESH)
    for peer in x_peers + z_peers + [sibling]:
        pl.semaphore_signal(barrier, inc=1, device_id={"rep": peer}, device_id_type=MESH)


    r_hi, r_lo, rt_hi, rt_lo, ones = (table.at[k * 256 : (k + 1) * 256] for k in range(5))
    l_pair, lt_pair, b_pair = (table.at[1280 + k * 128 : 1408 + k * 128] for k in range(3))
    l_lo, lt_lo = (table.at[1664:1792, k * 128 : (k + 1) * 128] for k in range(2))
    b_lo = table.at[1792:1920, 0:128]
    spread_ref = table.at[1920:1984]

    pull_own.wait()
    row = lax.broadcasted_iota(jnp.int32, (BLOCK, groups * BLOCK), 0)
    lane = lax.broadcasted_iota(jnp.int32, (BLOCK, groups * BLOCK), 1)
    own_slot = (lane & (BAND - 1)) == (row >> 2)
    for p in range(2):
        within = own_index[p : p + 1, :] & 255
        placed = jnp.where(own_slot, jnp.broadcast_to(within, own_slot.shape), 0).astype(f32)
        for g in range(groups):
            at = (2 * g + p) * BLOCK
            wide[at : at + BLOCK, :] = placed[:, g * BLOCK : (g + 1) * BLOCK].astype(bf16)
    pull_table.wait()

    mine = core * 32 + x * 8 + z

    @pl.loop(0, STEPS)
    def _(step):
        for copy in in_copies(step):
            copy.wait()
        at = columns(step)
        total = momentum_decay * acc[:, at] + grads[:, at].astype(f32)
        acc[:, at] = total
        stacked = jnp.concatenate([total[:, g * GROUP : (g + 1) * GROUP] for g in range(PER_STEP)], axis=0)
        half = times_right(stacked, r_hi, r_lo)
        coeff = jnp.concatenate(
            [times_left(l_pair, l_lo, half[g * 128 : (g + 1) * 128]) for g in range(PER_STEP)], axis=0
        )
        tall_at = pl.ds(pl.multiple_of(step * tall, tall), tall)
        index = dot(wide[tall_at, :], spread_ref[...])
        row = lax.broadcasted_iota(jnp.int32, (tall, GROUP), 0)
        lane = lax.broadcasted_iota(jnp.int32, (tall, GROUP), 1)
        place = (((row & 3) << 6) + (lane & 63)).astype(f32)
        kept = jnp.where(index == place, coeff, 0.0)
        kept_rows[tall_at, :] = kept
        hi, mid = split(kept)
        low = (kept - hi.astype(f32) - mid.astype(f32)).astype(bf16)
        sums = dot_nt(hi, spread_ref[...]) + (dot_nt(mid, spread_ref[...]) + dot_nt(low, spread_ref[...]))
        zrow = lax.broadcasted_iota(jnp.int32, (tall, BLOCK), 0)
        zlane = lax.broadcasted_iota(jnp.int32, (tall, BLOCK), 1)
        sums = jnp.where((zlane & (BAND - 1)) == ((zrow & 63) >> 2), sums, 0.0)
        for g in range(PER_STEP):
            pair = [
                jnp.sum(sums[(2 * g + p) * BLOCK : (2 * g + p + 1) * BLOCK], axis=0, keepdims=True)
                for p in range(2)
            ]
            rows[mine, pl.ds(step * PER_STEP + g, 1), :] = jnp.concatenate(pair, axis=1)

    def inverse_turn(step):
        half = times_right(kept_rows[pl.ds(pl.multiple_of(step * tall, tall), tall), :], rt_hi, rt_lo)
        for g in range(PER_STEP):
            at = pl.ds(pl.multiple_of(step * chunk + g * GROUP, GROUP), GROUP)
            acc[:, at] = acc[:, at] - times_left(lt_pair, lt_lo, half[g * 128 : (g + 1) * 128])
        fresh_copy(step).start()


    pl.semaphore_wait(barrier, 14)
    own = rows.at[mine]
    gz = [remote(own, own, gz_send.at[d], gz_recv.at[d], {"rep": peer}) for d, peer in enumerate(z_peers)]
    for copy in gz:
        copy.start()

    for pull in pulls:
        pull.wait()
    for p in range(2):
        for k in range((groups + 1) // 2):
            lanes = min(128, groups * BLOCK - k * 128)
            part = index_rows[:, :, :, p, k * 128 : k * 128 + lanes].reshape(64, lanes)
            turned = part.T & 255
            for b in range(lanes // BAND):
                at = (((2 * k + b // 4) * 2 + p) * 4 + b % 4) * 8
                places[at : at + 8, :] = jnp.concatenate(
                    [turned[b * 16 : b * 16 + 8], turned[b * 16 + 8 : b * 16 + 16]], axis=1
                )
    pl.loop(0, EARLY)(inverse_turn)

    for copy in gz:
        copy.wait()

    def bundle(of_x):
        return rows.at[pl.ds(core * 32 + of_x * 8, 8)]

    gx = [remote(bundle(x), bundle(x), gx_send.at[d], gx_recv.at[d], {"rep": peer}) for d, peer in enumerate(x_peers)]
    for copy in gx:
        copy.start()
    gs = [remote(bundle(x), bundle(x), gs_send.at[0], gs_recv.at[0], {"rep": sibling})]
    gs[0].start()
    pl.loop(EARLY, MIDDLE)(inverse_turn)
    for d in range(1, 4):
        gx[d - 1].wait_recv()
        part = bundle(lax.rem(x + 4 - d, 4))
        copy = remote(part, part, gs_send.at[d], gs_recv.at[d], {"rep": sibling})
        copy.start()
        gs.append(copy)
    for copy in gx:
        copy.wait_send()
    for copy in gs:
        copy.wait()


    def y_copies(unit):
        at = span(core, unit)
        parts = (
            (pl.ds(0, 32), at),
            (x_rows(x), at),
            z_part(z, unit),
        )
        return [
            remote(
                slots.at[0, rows_at, cols_at], slots.at[d + 1, rows_at, cols_at],
                y_send.at[unit, d, k], y_recv.at[unit, d, k], {"fsdp": y_peers[d]},
            )
            for d in range(3)
            for k, (rows_at, cols_at) in enumerate(parts)
        ]

    def x_rows(of_x):
        return pl.ds(pl.multiple_of(32 + of_x * 16, 16), 16)

    def z_part(of_z, unit):
        start = first_group(core, unit) * GROUP + (of_z % 4) * 128
        return pl.ds(pl.multiple_of(96 + (of_z // 4) * 16, 16), 16), pl.ds(pl.multiple_of(start, 128), 128)

    def onward_copies(unit, arriving):
        at = span(core, unit)
        out = []
        for d in range(3):
            part = slots.at[pl.ds(1, 3), x_rows(lax.rem(x + 3 - d, 4) if arriving else x), at]
            out.append(remote(part, part, x_send.at[unit, d], x_recv.at[unit, d], {"rep": x_peers[d]}))
        for d in range(7):
            rows_at, cols_at = z_part(lax.rem(z + 7 - d, 8) if arriving else z, unit)
            part = slots.at[pl.ds(1, 3), rows_at, cols_at]
            out.append(remote(part, part, z_send.at[unit, d], z_recv.at[unit, d], {"rep": z_peers[d]}))
        return out

    def s_copies(unit, at):
        return [
            remote(part, part, s_send.at[unit, k], s_recv.at[unit, k], {"rep": sibling})
            for k, part in enumerate((slots.at[:, :, at], updates.at[:, at]))
        ]

    def out_copies(sems, unit, at):
        out = [pltpu.make_async_copy(updates.at[:, at], update_out.at[:, at], sems.at[unit, 4])]
        for d in range(4):
            from_shard = lax.rem(shard + 4 - d, 4)
            place = pl.ds(pl.multiple_of(from_shard * cols + at.start, GROUP), at.size)
            out.append(pltpu.make_async_copy(slots.at[d, :, at], weights_out.at[:, place], sems.at[unit, d]))
        return out

    def by_width(of_core, unit, act):
        @pl.when(unit < UNITS - 1)
        def _():
            act(span(of_core, unit))

        @pl.when(unit == UNITS - 1)
        def _():
            act(last_span(of_core))

    tables = (rt_hi, rt_lo, b_pair, b_lo, ones)

    @pl.loop(0, UNITS + 3)
    def _(step):
        @pl.when(step < UNITS)
        def _():
            master_copy(step).wait()
            for k in range(2):
                g = first_group(core, step) + k
                turned = rows[:, g, :].T
                band = jnp.concatenate(
                    [
                        jnp.concatenate([turned[b * 16 : b * 16 + 8], turned[b * 16 + 8 : b * 16 + 16]], axis=1)
                        for b in range(8)
                    ],
                    axis=0,
                )
                lanes = pl.ds(pl.multiple_of(g * 64, 64), 64)
                at = pl.ds(pl.multiple_of(g * GROUP, GROUP), GROUP)
                update, weights = shared_group(band, places[lanes, :], masters[:, at], *tables)
                updates[:, at] = update
                slots[0, :, at] = weights
            for copy in y_copies(step):
                copy.start()

        @pl.when((step >= 1) & (step < UNITS + 1))
        def _():
            for copy in y_copies(step - 1):
                copy.wait_recv()
            for copy in onward_copies(step - 1, False):
                copy.start()

        @pl.when(step >= UNITS)
        def _():
            inverse_turn(MIDDLE + step - UNITS)

        @pl.when((step >= 2) & (step < UNITS + 2))
        def _():
            unit = step - 2
            for copy in onward_copies(unit, True):
                copy.wait_recv()

            def act(at):
                for copy in s_copies(unit, at):
                    copy.start()

            by_width(core, unit, act)
            for copy in out_copies(o_sem, unit, span(core, unit)):
                copy.start()

        @pl.when(step >= 3)
        def _():
            unit = step - 3

            def act(at):
                for copy in s_copies(unit, at):
                    copy.wait_recv()
                for copy in out_copies(t_sem, unit, at):
                    copy.start()

            by_width(1 - core, unit, act)

    @pl.loop(0, STEPS)
    def _(step):
        fresh_copy(step).wait()

    @pl.loop(0, UNITS)
    def _(unit):
        for copy in y_copies(unit) + onward_copies(unit, False):
            copy.wait_send()
        for copy in out_copies(o_sem, unit, span(core, unit)):
            copy.wait()

        def drain_own(at):
            for copy in s_copies(unit, at):
                copy.wait_send()

        def drain_other(at):
            for copy in out_copies(t_sem, unit, at):
                copy.wait()

        by_width(core, unit, drain_own)
        by_width(1 - core, unit, drain_other)


def table_array():
    t = TABLES
    beside = lambda a, b: np.concatenate([a, b], axis=1)
    parts = [
        *t["right"], *t["right_t"], t["ones"], t["left"][0], t["left_t"][0], t["back"][0],
        beside(t["left"][1], t["left_t"][1]), beside(t["back"][1], t["back"][1]), t["spread"],
    ]
    return jnp.asarray(np.concatenate(parts, axis=0))


def shards(grads, momentum, master, band_index):
    rows, cols = master.shape
    reps, _, lanes = band_index.shape
    groups = cols // GROUP
    dma = pltpu.SemaphoreType.DMA
    table = table_array()
    anywhere = pl.BlockSpec(memory_space=pl.ANY)
    vmem = pltpu.VMEM
    return tuple(pl.pallas_call(
        kernel,
        in_specs=[anywhere] * 5,
        out_specs=[anywhere] * 3,
        out_shape=[
            jax.ShapeDtypeStruct(momentum.shape, f32),
            jax.ShapeDtypeStruct(master.shape, f32),
            jax.ShapeDtypeStruct((rows, 4 * cols), bf16),
        ],
        scratch_shapes=[
            vmem((rows, cols), bf16),
            vmem((rows, cols), f32),
            vmem((groups * rows, GROUP), f32),
            vmem((groups * rows, BLOCK), bf16),
            vmem((2, lanes), jnp.int32),
            vmem((2, 4, 8, 2, lanes), jnp.int32),
            vmem((groups * 64, 128), jnp.int32),
            vmem((reps, groups, 128), f32),
            vmem((rows, cols), f32),
            vmem((rows, cols), f32),
            vmem((4, rows, cols), bf16),
            vmem(table.shape, bf16),
            dma((STEPS, 2)), dma((4,)), dma((STEPS,)),
            dma((7,)), dma((7,)), dma((3,)), dma((3,)), dma((4,)), dma((4,)),
            dma((UNITS,)), dma((UNITS, 3, 3)), dma((UNITS, 3, 3)), dma((UNITS, 3)), dma((UNITS, 3)),
            dma((UNITS, 7)), dma((UNITS, 7)), dma((UNITS, 2)), dma((UNITS, 2)), dma((UNITS, 5)), dma((UNITS, 5)),
        ],
        compiler_params=pltpu.CompilerParams(
            collective_id=0, has_side_effects=True, vmem_limit_bytes=VMEM_LIMIT
        ),
    )(grads, momentum, band_index.reshape(4, 8, 2, 2, lanes), master, table))


def solution(mesh):
    in_specs = (
        P("rep", None, "fsdp"),
        P("rep", None, "fsdp"),
        P(None, "fsdp"),
        P(None, None, "fsdp"),
    )
    out_specs = (P("rep", None, "fsdp"), P(None, "fsdp"), P())
    return jax.shard_map(shards, mesh=mesh, in_specs=in_specs, out_specs=out_specs, check_vma=False)
```

time: 210 us -> 87.7 us (0.42)
  waiting for transfers between devices: 72.2 us -> 0 us
  blocking collectives: 55 us -> 0 us
  Pallas kernels: 46.8 us -> 75.5 us
  between operations: 14.2 us -> 0.65 us
  local copies, waits for them, and re-layouts: 21.7 us -> 11.4 us
    all_gather x1 -> x0, waiting for transfers between devices: 72.2 us -> none  [shards(): weights_full = lax.all_gather(weights_local, 'fsdp', axis=1, tiled=True)]
    all_gather x1 -> x0, blocking collectives: 55 us -> none  [shards(): bands = lax.all_gather(band, 'rep', axis=0, tiled=True)]
    pallas_call x2 -> x1, Pallas kernels: 46.8 us -> 75.5 us  [shards(): pl.pallas_call(kernel, in_specs=[anywhere] * 5, out_specs=[anywhere] * 3,...]
    reshape x2 -> x0, local copies, waits for them, and re-layouts: 4.69 us -> none  [the longest x1 2.59 us: by_group(): return split_up.transpose(0, 2, 1, 3).reshape(reps, 2 * lanes)]
    transpose x1 -> x0, local copies, waits for them, and re-layouts: 4.52 us -> none  [by_group(): return split_up.transpose(0, 2, 1, 3).reshape(reps, 2 * lanes)]
    unnamed x37 -> x7, local copies, waits for them, and re-layouts: 12.5 us -> 11.4 us
  transfers between devices with their start and end apart: 1 -> 0, of which waited for: 1 -> 0; matrix products, arithmetic and copies ran while one was open for 0% -> 0% of each run, Pallas kernels for 0% -> 0%
where the time goes in v3:
time: 87.7 us; the launch traced here: 87.6 us
  Pallas kernels  75.5 us (86%)
  local copies, waits for them, and re-layouts  11.4 us (13%)
    pallas_call x1, Pallas kernels, shards(): pl.pallas_call(kernel, in_specs=[anywhere] * 5, out_specs=[anywhere] * 3,...  75.5 us
    unnamed x7, local copies, waits for them, and re-layouts  11.4 us

profile of v3, /device:TPU:1, one launch (start us, length us, event | category | flops | bytes accessed | tf_op | source)
XLA Modules:
  0.0 87.6 jit_solution(17554151649562204001)
XLA Ops:
  0.6 75.5 %shard_map.76 = (f32[1,128,6912]{2,1,0:T(8,128)}, f32[128,6912]{1,0:T(8,128)}, bf16[128,27648]{1,0:T(8,128)(2,1)}) custom-call(bf16[1,128,6912]{2,1,0:T(8,128)(2,1)} %grads_ref.1, f32[1,128,6912]{2,1,0:T(8,128)} %mom_ref.1, s32[4,8,2,2,1728]{4,3,2,1,0:T(2,128)} %bitcast.1, f32[128,6912]{1,0:T(8,128)} %master_ref.1, bf16[1984,256]{1,0:T(8,128)(2,1)} %constant.2.clone.table_ref), custom_call_target="tpu_custom_call" | custom-call | tf_op jit(solution)/shard_map/pallas_call | solution.py:504
  76.1 0.0 copy-start.1
  76.1 4.2 %copy.11 = f32[1,128,6912]{2,1,0:T(8,128)} copy(f32[1,128,6912]{2,1,0:T(8,128)} %get-tuple-element.6) | data formatting | bytes 7077888
  80.3 0.0 copy-done.1
  80.3 0.0 copy-start
  80.3 1.8 %copy.12 = f32[128,6912]{1,0:T(8,128)} copy(f32[128,6912]{1,0:T(8,128)S(1)} %copy-done.1) | data formatting | bytes 7077888
  82.1 2.5 %copy-done = bf16[128,27648]{1,0:T(8,128)(2,1)S(1)} copy-done((bf16[128,27648]{1,0:T(8,128)(2,1)S(1)}, bf16[128,27648]{1,0:T(8,128)(2,1)}, u32[]{:S(2)}) %copy-start) | copy-done | bytes 7077912
  84.6 3.0 %copy.13 = bf16[128,27648]{1,0:T(8,128)(2,1)} copy(bf16[128,27648]{1,0:T(8,128)(2,1)S(1)} %copy-done) | data formatting | bytes 14155776
Async XLA Ops:
  76.1 4.2 %copy-start.1 = (f32[128,6912]{1,0:T(8,128)S(1)}, f32[128,6912]{1,0:T(8,128)}, u32[]{:S(2)}) copy-start(f32[128,6912]{1,0:T(8,128)} %get-tuple-element.7) | copy-start | bytes 10616836
  80.3 4.3 %copy-start = (bf16[128,27648]{1,0:T(8,128)(2,1)S(1)}, bf16[128,27648]{1,0:T(8,128)(2,1)}, u32[]{:S(2)}) copy-start(bf16[128,27648]{1,0:T(8,128)(2,1)} %get-tuple-element.8) | copy-start | bytes 21233668

commit v4 on v3

--- a/solution.py
+++ b/solution.py
@@ -155,6 +155,7 @@
 
 UNITS = 7
 WIDE = 2 * GROUP
+Y_AFTER, ONWARD_AFTER, SWAP_AFTER = 2, 4, 6
 STEPS = 9
 EARLY, MIDDLE = 2, 6
 
@@ -400,7 +401,7 @@
 
     tables = (rt_hi, rt_lo, b_pair, b_lo, ones)
 
-    @pl.loop(0, UNITS + 3)
+    @pl.loop(0, UNITS + SWAP_AFTER)
     def _(step):
         @pl.when(step < UNITS)
         def _():
@@ -423,20 +424,20 @@
             for copy in y_copies(step):
                 copy.start()
 
-        @pl.when((step >= 1) & (step < UNITS + 1))
-        def _():
-            for copy in y_copies(step - 1):
+        @pl.when((step >= Y_AFTER) & (step < UNITS + Y_AFTER))
+        def _():
+            for copy in y_copies(step - Y_AFTER):
                 copy.wait_recv()
-            for copy in onward_copies(step - 1, False):
+            for copy in onward_copies(step - Y_AFTER, False):
                 copy.start()
 
-        @pl.when(step >= UNITS)
+        @pl.when((step >= UNITS) & (step < UNITS + STEPS - MIDDLE))
         def _():
             inverse_turn(MIDDLE + step - UNITS)
 
-        @pl.when((step >= 2) & (step < UNITS + 2))
-        def _():
-            unit = step - 2
+        @pl.when((step >= ONWARD_AFTER) & (step < UNITS + ONWARD_AFTER))
+        def _():
+            unit = step - ONWARD_AFTER
             for copy in onward_copies(unit, True):
                 copy.wait_recv()
 
@@ -448,9 +449,9 @@
             for copy in out_copies(o_sem, unit, span(core, unit)):
                 copy.start()
 
-        @pl.when(step >= 3)
-        def _():
-            unit = step - 3
+        @pl.when(step >= SWAP_AFTER)
+        def _():
+            unit = step - SWAP_AFTER
 
             def act(at):
                 for copy in s_copies(unit, at):

time: 87.7 us -> 79.9 us (0.911)
  Pallas kernels: 75.5 us -> 67.7 us
    pallas_call x1, Pallas kernels: 75.5 us -> 67.7 us  [shards(): pl.pallas_call(kernel, in_specs=[anywhere] * 5, out_specs=[anywhere] * 3,...]
where the time goes in v4:
time: 79.9 us; the launch traced here: 79.7 us
  Pallas kernels  67.7 us (85%)
  local copies, waits for them, and re-layouts  11.4 us (14%)
    pallas_call x1, Pallas kernels, shards(): pl.pallas_call(kernel, in_specs=[anywhere] * 5, out_specs=[anywhere] * 3,...  67.7 us
    unnamed x7, local copies, waits for them, and re-layouts  11.4 us

profile of v4, /device:TPU:1, one launch (start us, length us, event | category | flops | bytes accessed | tf_op | source)
XLA Modules:
  0.0 79.7 jit_solution(570585733172940305)
XLA Ops:
  0.6 67.7 %shard_map.76 = (f32[1,128,6912]{2,1,0:T(8,128)}, f32[128,6912]{1,0:T(8,128)}, bf16[128,27648]{1,0:T(8,128)(2,1)}) custom-call(bf16[1,128,6912]{2,1,0:T(8,128)(2,1)} %grads_ref.1, f32[1,128,6912]{2,1,0:T(8,128)} %mom_ref.1, s32[4,8,2,2,1728]{4,3,2,1,0:T(2,128)} %bitcast.1, f32[128,6912]{1,0:T(8,128)} %master_ref.1, bf16[1984,256]{1,0:T(8,128)(2,1)} %constant.2.clone.table_ref), custom_call_target="tpu_custom_call" | custom-call | tf_op jit(solution)/shard_map/pallas_call | solution.py:505
  68.3 0.0 copy-start.1
  68.3 4.2 %copy.11 = f32[1,128,6912]{2,1,0:T(8,128)} copy(f32[1,128,6912]{2,1,0:T(8,128)} %get-tuple-element.6) | data formatting | bytes 7077888
  72.5 0.0 copy-done.1
  72.5 0.0 copy-start
  72.5 1.8 %copy.12 = f32[128,6912]{1,0:T(8,128)} copy(f32[128,6912]{1,0:T(8,128)S(1)} %copy-done.1) | data formatting | bytes 7077888
  74.3 2.5 %copy-done = bf16[128,27648]{1,0:T(8,128)(2,1)S(1)} copy-done((bf16[128,27648]{1,0:T(8,128)(2,1)S(1)}, bf16[128,27648]{1,0:T(8,128)(2,1)}, u32[]{:S(2)}) %copy-start) | copy-done | bytes 7077912
  76.8 3.0 %copy.13 = bf16[128,27648]{1,0:T(8,128)(2,1)} copy(bf16[128,27648]{1,0:T(8,128)(2,1)S(1)} %copy-done) | data formatting | bytes 14155776
Async XLA Ops:
  68.3 4.2 %copy-start.1 = (f32[128,6912]{1,0:T(8,128)S(1)}, f32[128,6912]{1,0:T(8,128)}, u32[]{:S(2)}) copy-start(f32[128,6912]{1,0:T(8,128)} %get-tuple-element.7) | copy-start | bytes 10616836
  72.5 4.3 %copy-start = (bf16[128,27648]{1,0:T(8,128)(2,1)S(1)}, bf16[128,27648]{1,0:T(8,128)(2,1)}, u32[]{:S(2)}) copy-start(bf16[128,27648]{1,0:T(8,128)(2,1)} %get-tuple-element.8) | copy-start | bytes 21233668

commit v5 on v4

--- a/solution.py
+++ b/solution.py
@@ -18,7 +18,7 @@
 bf16 = jnp.bfloat16
 f32 = jnp.float32
 MESH = pl.DeviceIdType.MESH
-VMEM_LIMIT = 60 * 2**20
+VMEM_LIMIT = 46 * 2**20
 
 
 def dct64():
@@ -162,10 +162,10 @@
 
 def kernel(
     grads_ref, mom_ref, index_ref, master_ref, table_ref,
-    fresh_out, update_out, weights_out,
-    grads, acc, kept_rows, wide, own_index, index_rows, places, rows, masters, updates, slots, table,
-    in_sem, index_sem, f_sem, gz_send, gz_recv, gx_send, gx_recv, gs_send, gs_recv,
-    m_sem, y_send, y_recv, x_send, x_recv, z_send, z_recv, s_send, s_recv, o_sem, t_sem,
+    acc, updates, slots,
+    grads, kept_rows, wide, own_index, index_rows, places, rows, masters, table,
+    in_sem, index_sem, gz_send, gz_recv, gx_send, gx_recv, gs_send, gs_recv,
+    m_sem, y_send, y_recv, x_send, x_recv, z_send, z_recv, s_send, s_recv,
 ):
     rep = lax.axis_index("rep")
     shard = lax.axis_index("fsdp")
@@ -194,10 +194,6 @@
             pltpu.make_async_copy(grads_ref.at[0, :, at], grads.at[:, at], in_sem.at[step, 0]),
             pltpu.make_async_copy(mom_ref.at[0, :, at], acc.at[:, at], in_sem.at[step, 1]),
         )
-
-    def fresh_copy(step):
-        at = columns(step)
-        return pltpu.make_async_copy(acc.at[:, at], fresh_out.at[0, :, at], f_sem.at[step])
 
     def first_group(of_core, unit):
         return 2 * unit + of_core * (groups - 2 - 4 * unit)
@@ -277,8 +273,7 @@
         kept = jnp.where(index == place, coeff, 0.0)
         kept_rows[tall_at, :] = kept
         hi, mid = split(kept)
-        low = (kept - hi.astype(f32) - mid.astype(f32)).astype(bf16)
-        sums = dot_nt(hi, spread_ref[...]) + (dot_nt(mid, spread_ref[...]) + dot_nt(low, spread_ref[...]))
+        sums = dot_nt(hi, spread_ref[...]) + dot_nt(mid, spread_ref[...])
         zrow = lax.broadcasted_iota(jnp.int32, (tall, BLOCK), 0)
         zlane = lax.broadcasted_iota(jnp.int32, (tall, BLOCK), 1)
         sums = jnp.where((zlane & (BAND - 1)) == ((zrow & 63) >> 2), sums, 0.0)
@@ -294,7 +289,6 @@
         for g in range(PER_STEP):
             at = pl.ds(pl.multiple_of(step * chunk + g * GROUP, GROUP), GROUP)
             acc[:, at] = acc[:, at] - times_left(lt_pair, lt_lo, half[g * 128 : (g + 1) * 128])
-        fresh_copy(step).start()
 
 
     pl.semaphore_wait(barrier, 14)
@@ -381,14 +375,6 @@
             remote(part, part, s_send.at[unit, k], s_recv.at[unit, k], {"rep": sibling})
             for k, part in enumerate((slots.at[:, :, at], updates.at[:, at]))
         ]
-
-    def out_copies(sems, unit, at):
-        out = [pltpu.make_async_copy(updates.at[:, at], update_out.at[:, at], sems.at[unit, 4])]
-        for d in range(4):
-            from_shard = lax.rem(shard + 4 - d, 4)
-            place = pl.ds(pl.multiple_of(from_shard * cols + at.start, GROUP), at.size)
-            out.append(pltpu.make_async_copy(slots.at[d, :, at], weights_out.at[:, place], sems.at[unit, d]))
-        return out
 
     def by_width(of_core, unit, act):
         @pl.when(unit < UNITS - 1)
@@ -446,8 +432,6 @@
                     copy.start()
 
             by_width(core, unit, act)
-            for copy in out_copies(o_sem, unit, span(core, unit)):
-                copy.start()
 
         @pl.when(step >= SWAP_AFTER)
         def _():
@@ -456,32 +440,19 @@
             def act(at):
                 for copy in s_copies(unit, at):
                     copy.wait_recv()
-                for copy in out_copies(t_sem, unit, at):
-                    copy.start()
 
             by_width(1 - core, unit, act)
-
-    @pl.loop(0, STEPS)
-    def _(step):
-        fresh_copy(step).wait()
 
     @pl.loop(0, UNITS)
     def _(unit):
         for copy in y_copies(unit) + onward_copies(unit, False):
             copy.wait_send()
-        for copy in out_copies(o_sem, unit, span(core, unit)):
-            copy.wait()
 
         def drain_own(at):
             for copy in s_copies(unit, at):
                 copy.wait_send()
 
-        def drain_other(at):
-            for copy in out_copies(t_sem, unit, at):
-                copy.wait()
-
         by_width(core, unit, drain_own)
-        by_width(1 - core, unit, drain_other)
 
 
 def table_array():
@@ -494,6 +465,46 @@
     return jnp.asarray(np.concatenate(parts, axis=0))
 
 
+def settle(fresh, update, slots):
+    rows, cols = update.shape
+    part = cols // 9
+
+    def body(fresh_ref, update_ref, slots_ref, fresh_out, update_out, weights_out, sem):
+        shard = lax.axis_index("fsdp")
+        copies = []
+        for n in range(9):
+            at = slice(n * part, (n + 1) * part)
+            copies.append(pltpu.make_async_copy(fresh_ref.at[:, at], fresh_out.at[0, :, at], sem.at[n, 0]))
+            copies.append(pltpu.make_async_copy(update_ref.at[:, at], update_out.at[:, at], sem.at[n, 1]))
+        for d in range(4):
+            from_shard = lax.rem(shard + 4 - d, 4)
+            for n in range(3):
+                start = pl.multiple_of(from_shard * cols + n * 3 * part, GROUP)
+                copies.append(pltpu.make_async_copy(
+                    slots_ref.at[d, :, n * 3 * part : (n + 1) * 3 * part],
+                    weights_out.at[:, pl.ds(start, 3 * part)],
+                    sem.at[d * 3 + n, 2],
+                ))
+        for copy in copies:
+            copy.start()
+        for copy in copies:
+            copy.wait()
+
+    anywhere = pl.BlockSpec(memory_space=pl.ANY)
+    return tuple(pl.pallas_call(
+        body,
+        in_specs=[anywhere] * 3,
+        out_specs=[anywhere] * 3,
+        out_shape=[
+            jax.ShapeDtypeStruct((1, rows, cols), f32),
+            jax.ShapeDtypeStruct((rows, cols), f32),
+            jax.ShapeDtypeStruct((rows, 4 * cols), bf16),
+        ],
+        scratch_shapes=[pltpu.SemaphoreType.DMA((12, 3))],
+        compiler_params=pltpu.CompilerParams(vmem_limit_bytes=2 * 2**20),
+    )(fresh, update, slots))
+
+
 def shards(grads, momentum, master, band_index):
     rows, cols = master.shape
     reps, _, lanes = band_index.shape
@@ -502,18 +513,13 @@
     table = table_array()
     anywhere = pl.BlockSpec(memory_space=pl.ANY)
     vmem = pltpu.VMEM
-    return tuple(pl.pallas_call(
+    return settle(*pl.pallas_call(
         kernel,
         in_specs=[anywhere] * 5,
-        out_specs=[anywhere] * 3,
-        out_shape=[
-            jax.ShapeDtypeStruct(momentum.shape, f32),
-            jax.ShapeDtypeStruct(master.shape, f32),
-            jax.ShapeDtypeStruct((rows, 4 * cols), bf16),
-        ],
+        out_specs=[pl.BlockSpec(memory_space=vmem)] * 3,
+        out_shape=[vmem((rows, cols), f32), vmem((rows, cols), f32), vmem((4, rows, cols), bf16)],
         scratch_shapes=[
             vmem((rows, cols), bf16),
-            vmem((rows, cols), f32),
             vmem((groups * rows, GROUP), f32),
             vmem((groups * rows, BLOCK), bf16),
             vmem((2, lanes), jnp.int32),
@@ -521,13 +527,11 @@
             vmem((groups * 64, 128), jnp.int32),
             vmem((reps, groups, 128), f32),
             vmem((rows, cols), f32),
-            vmem((rows, cols), f32),
-            vmem((4, rows, cols), bf16),
             vmem(table.shape, bf16),
-            dma((STEPS, 2)), dma((4,)), dma((STEPS,)),
+            dma((STEPS, 2)), dma((4,)),
             dma((7,)), dma((7,)), dma((3,)), dma((3,)), dma((4,)), dma((4,)),
             dma((UNITS,)), dma((UNITS, 3, 3)), dma((UNITS, 3, 3)), dma((UNITS, 3)), dma((UNITS, 3)),
-            dma((UNITS, 7)), dma((UNITS, 7)), dma((UNITS, 2)), dma((UNITS, 2)), dma((UNITS, 5)), dma((UNITS, 5)),
+            dma((UNITS, 7)), dma((UNITS, 7)), dma((UNITS, 2)), dma((UNITS, 2)),
         ],
         compiler_params=pltpu.CompilerParams(
             collective_id=0, has_side_effects=True, vmem_limit_bytes=VMEM_LIMIT

time: 79.9 us -> 71.7 us (0.90)
  local copies, waits for them, and re-layouts: 11.4 us -> 0 us
  Pallas kernels: 67.7 us -> 70.9 us
    unnamed x7 -> x0, local copies, waits for them, and re-layouts: 11.4 us -> none
    pallas_call x1 -> x2, Pallas kernels: 67.7 us -> 70.9 us  [the longest x1 65.5 us: shards(): pl.pallas_call(kernel, in_specs=[anywhere] * 5, out_specs=[pl.BlockSpec(m...]
where the time goes in v5:
time: 71.7 us; the launch traced here: 71.5 us
  Pallas kernels  70.9 us (99%)
    pallas_call x1, Pallas kernels, shards(): pl.pallas_call(kernel, in_specs=[anywhere] * 5, out_specs=[pl.BlockSpec(m...  65.5 us
    pallas_call x1, Pallas kernels, settle(): pl.pallas_call(body, in_specs=[anywhere] * 3, out_specs=[anywhere] * 3, o...  5.33 us

profile of v5, /device:TPU:1, one launch (start us, length us, event | category | flops | bytes accessed | tf_op | source)
XLA Modules:
  0.0 71.5 jit_solution(16338956918703196639)
XLA Ops:
  0.6 65.5 %shard_map.76 = (f32[128,6912]{1,0:T(8,128)S(1)}, f32[128,6912]{1,0:T(8,128)S(1)}, bf16[4,128,6912]{2,1,0:T(8,128)(2,1)S(1)}) custom-call(bf16[1,128,6912]{2,1,0:T(8,128)(2,1)} %grads_ref.1, f32[1,128,6912]{2,1,0:T(8,128)} %mom_ref.1, s32[4,8,2,2,1728]{4,3,2,1,0:T(2,128)} %bitcast.1, f32[128,6912]{1,0:T(8,128)} %master_ref.1, ...), custom_call_target="tpu_custom_call" | custom-call | tf_op jit(solution)/shard_map/pallas_call | solution.py:516
  66.2 5.3 %shard_map.77 = (f32[1,128,6912]{2,1,0:T(8,128)}, f32[128,6912]{1,0:T(8,128)}, bf16[128,27648]{1,0:T(8,128)(2,1)}) custom-call(f32[128,6912]{1,0:T(8,128)S(1)} %get-tuple-element.6.fresh_ref, f32[128,6912]{1,0:T(8,128)S(1)} %get-tuple-element.7.update_ref, bf16[4,128,6912]{2,1,0:T(8,128)(2,1)S(1)} %get-tuple-element.8.slots_ref), custom_call_target="tpu_custom_call" | custom-call | tf_op jit(solution)/shard_map/pallas_call | solution.py:494

commit v6 on v5

--- a/solution.py
+++ b/solution.py
@@ -145,6 +145,11 @@
     return update, (master - learn_rate * update).astype(bf16)
 
 
+def sent_place(g):
+    from_8, from_19 = (g + 24) // 32, (g + 5) // 24
+    return g + 8 * from_8 + from_19 * (26 - 2 * g)
+
+
 def rep_parts(r):
     return r // 16, (r // 2) % 8, r % 2
 
@@ -282,7 +287,7 @@
                 jnp.sum(sums[(2 * g + p) * BLOCK : (2 * g + p + 1) * BLOCK], axis=0, keepdims=True)
                 for p in range(2)
             ]
-            rows[mine, pl.ds(step * PER_STEP + g, 1), :] = jnp.concatenate(pair, axis=1)
+            rows[mine, pl.ds(sent_place(step * PER_STEP + g), 1), :] = jnp.concatenate(pair, axis=1)
 
     def inverse_turn(step):
         half = times_right(kept_rows[pl.ds(pl.multiple_of(step * tall, tall), tall), :], rt_hi, rt_lo)
@@ -292,10 +297,35 @@
 
 
     pl.semaphore_wait(barrier, 14)
-    own = rows.at[mine]
-    gz = [remote(own, own, gz_send.at[d], gz_recv.at[d], {"rep": peer}) for d, peer in enumerate(z_peers)]
-    for copy in gz:
-        copy.start()
+    halves_at = (pl.ds(0, 16), pl.ds(16, groups - 16))
+
+    def z_band_copies(h):
+        own = rows.at[mine, halves_at[h]]
+        return [
+            remote(own, own, gz_send.at[h, d], gz_recv.at[h, d], {"rep": peer}) for d, peer in enumerate(z_peers)
+        ]
+
+    def bundle(of_x, h):
+        return rows.at[pl.ds(core * 32 + of_x * 8, 8), halves_at[h]]
+
+    def x_band_copies(h):
+        part = bundle(x, h)
+        return [
+            remote(part, part, gx_send.at[h, d], gx_recv.at[h, d], {"rep": peer}) for d, peer in enumerate(x_peers)
+        ]
+
+    def s_band_copy(h, d):
+        part = bundle(lax.rem(x + 4 - d, 4), h)
+        return remote(part, part, gs_send.at[h, d], gs_recv.at[h, d], {"rep": sibling})
+
+    def pass_on(h):
+        for d, copy in enumerate(x_band_copies(h)):
+            copy.wait_recv()
+            s_band_copy(h, d + 1).start()
+
+    for h in range(2):
+        for copy in z_band_copies(h):
+            copy.start()
 
     for pull in pulls:
         pull.wait()
@@ -311,28 +341,16 @@
                 )
     pl.loop(0, EARLY)(inverse_turn)
 
-    for copy in gz:
-        copy.wait()
-
-    def bundle(of_x):
-        return rows.at[pl.ds(core * 32 + of_x * 8, 8)]
-
-    gx = [remote(bundle(x), bundle(x), gx_send.at[d], gx_recv.at[d], {"rep": peer}) for d, peer in enumerate(x_peers)]
-    for copy in gx:
-        copy.start()
-    gs = [remote(bundle(x), bundle(x), gs_send.at[0], gs_recv.at[0], {"rep": sibling})]
-    gs[0].start()
+    for h in range(2):
+        for copy in z_band_copies(h):
+            copy.wait()
+        for copy in x_band_copies(h):
+            copy.start()
+        s_band_copy(h, 0).start()
     pl.loop(EARLY, MIDDLE)(inverse_turn)
-    for d in range(1, 4):
-        gx[d - 1].wait_recv()
-        part = bundle(lax.rem(x + 4 - d, 4))
-        copy = remote(part, part, gs_send.at[d], gs_recv.at[d], {"rep": sibling})
-        copy.start()
-        gs.append(copy)
-    for copy in gx:
-        copy.wait_send()
-    for copy in gs:
-        copy.wait()
+    pass_on(0)
+    for d in range(4):
+        s_band_copy(0, d).wait()
 
 
     def y_copies(unit):
@@ -389,12 +407,23 @@
 
     @pl.loop(0, UNITS + SWAP_AFTER)
     def _(step):
+        @pl.when(step == 1)
+        def _():
+            pass_on(1)
+
+        @pl.when(step == 4)
+        def _():
+            for d in range(4):
+                s_band_copy(1, d).wait()
+
         @pl.when(step < UNITS)
         def _():
             master_copy(step).wait()
+            later = step // 4
             for k in range(2):
                 g = first_group(core, step) + k
-                turned = rows[:, g, :].T
+                early_place = 2 * step + k + core * (9 - 2 * k)
+                turned = rows[:, (1 - later) * early_place + later * (g + 8), :].T
                 band = jnp.concatenate(
                     [
                         jnp.concatenate([turned[b * 16 : b * 16 + 8], turned[b * 16 + 8 : b * 16 + 16]], axis=1)
@@ -442,6 +471,10 @@
                     copy.wait_recv()
 
             by_width(1 - core, unit, act)
+
+    for h in range(2):
+        for copy in x_band_copies(h):
+            copy.wait_send()
 
     @pl.loop(0, UNITS)
     def _(unit):
@@ -529,7 +562,7 @@
             vmem((rows, cols), f32),
             vmem(table.shape, bf16),
             dma((STEPS, 2)), dma((4,)),
-            dma((7,)), dma((7,)), dma((3,)), dma((3,)), dma((4,)), dma((4,)),
+            dma((2, 7)), dma((2, 7)), dma((2, 3)), dma((2, 3)), dma((2, 4)), dma((2, 4)),
             dma((UNITS,)), dma((UNITS, 3, 3)), dma((UNITS, 3, 3)), dma((UNITS, 3)), dma((UNITS, 3)),
             dma((UNITS, 7)), dma((UNITS, 7)), dma((UNITS, 2)), dma((UNITS, 2)),
         ],

time: 71.7 us -> 69.5 us (0.969)
  Pallas kernels: 70.9 us -> 68.7 us
    pallas_call x1, Pallas kernels: 65.5 us -> 63.4 us  [shards(): pl.pallas_call(kernel, in_specs=[anywhere] * 5, out_specs=[pl.BlockSpec(m...]
where the time goes in v6:
time: 69.5 us; the launch traced here: 69.4 us
  Pallas kernels  68.7 us (99%)
    pallas_call x1, Pallas kernels, shards(): pl.pallas_call(kernel, in_specs=[anywhere] * 5, out_specs=[pl.BlockSpec(m...  63.4 us
    pallas_call x1, Pallas kernels, settle(): pl.pallas_call(body, in_specs=[anywhere] * 3, out_specs=[anywhere] * 3, o...  5.33 us

profile of v6, /device:TPU:1, one launch (start us, length us, event | category | flops | bytes accessed | tf_op | source)
XLA Modules:
  0.0 69.4 jit_solution(10486610699546741482)
XLA Ops:
  0.6 63.4 %shard_map.76 = (f32[128,6912]{1,0:T(8,128)S(1)}, f32[128,6912]{1,0:T(8,128)S(1)}, bf16[4,128,6912]{2,1,0:T(8,128)(2,1)S(1)}) custom-call(bf16[1,128,6912]{2,1,0:T(8,128)(2,1)} %grads_ref.1, f32[1,128,6912]{2,1,0:T(8,128)} %mom_ref.1, s32[4,8,2,2,1728]{4,3,2,1,0:T(2,128)} %bitcast.1, f32[128,6912]{1,0:T(8,128)} %master_ref.1, ...), custom_call_target="tpu_custom_call" | custom-call | tf_op jit(solution)/shard_map/pallas_call | solution.py:549
  64.0 5.3 %shard_map.77 = (f32[1,128,6912]{2,1,0:T(8,128)}, f32[128,6912]{1,0:T(8,128)}, bf16[128,27648]{1,0:T(8,128)(2,1)}) custom-call(f32[128,6912]{1,0:T(8,128)S(1)} %get-tuple-element.6.fresh_ref, f32[128,6912]{1,0:T(8,128)S(1)} %get-tuple-element.7.update_ref, bf16[4,128,6912]{2,1,0:T(8,128)(2,1)S(1)} %get-tuple-element.8.slots_ref), custom_call_target="tpu_custom_call" | custom-call | tf_op jit(solution)/shard_map/pallas_call | solution.py:527

commit v7 on v6

--- a/solution.py
+++ b/solution.py
@@ -127,9 +127,8 @@
     return jnp.concatenate(parts, axis=0)
 
 
-def shared_group(band, index, master, rt_hi, rt_lo, b_pair, b_lo, ones_ref):
-    total = summed_coefficients(band, index)
-    direction = times_left(b_pair, b_lo, times_right(total, rt_hi, rt_lo))
+def shared_group(half, master, b_pair, b_lo, ones_ref):
+    direction = times_left(b_pair, b_lo, half)
     square = direction * direction
     sums = [
         jnp.broadcast_to(jnp.sum(square[p * BLOCK : (p + 1) * BLOCK], axis=0, keepdims=True), (8, GROUP))
@@ -403,8 +402,6 @@
         def _():
             act(last_span(of_core))
 
-    tables = (rt_hi, rt_lo, b_pair, b_lo, ones)
-
     @pl.loop(0, UNITS + SWAP_AFTER)
     def _(step):
         @pl.when(step == 1)
@@ -420,6 +417,7 @@
         def _():
             master_copy(step).wait()
             later = step // 4
+            totals = []
             for k in range(2):
                 g = first_group(core, step) + k
                 early_place = 2 * step + k + core * (9 - 2 * k)
@@ -432,8 +430,13 @@
                     axis=0,
                 )
                 lanes = pl.ds(pl.multiple_of(g * 64, 64), 64)
-                at = pl.ds(pl.multiple_of(g * GROUP, GROUP), GROUP)
-                update, weights = shared_group(band, places[lanes, :], masters[:, at], *tables)
+                totals.append(summed_coefficients(band, places[lanes, :]))
+            halves_of = times_right(jnp.concatenate(totals, axis=0), rt_hi, rt_lo)
+            for k in range(2):
+                at = pl.ds(pl.multiple_of((first_group(core, step) + k) * GROUP, GROUP), GROUP)
+                update, weights = shared_group(
+                    halves_of[k * 2 * BLOCK : (k + 1) * 2 * BLOCK], masters[:, at], b_pair, b_lo, ones
+                )
                 updates[:, at] = update
                 slots[0, :, at] = weights
             for copy in y_copies(step):

time: 69.5 us -> 69.1 us (level)
  no operation moved by 1% of the time
where the time goes in v7:
time: 69.1 us; the launch traced here: 68.9 us
  Pallas kernels  68.3 us (99%)
    pallas_call x1, Pallas kernels, shards(): pl.pallas_call(kernel, in_specs=[anywhere] * 5, out_specs=[pl.BlockSpec(m...  62.9 us
    pallas_call x1, Pallas kernels, settle(): pl.pallas_call(body, in_specs=[anywhere] * 3, out_specs=[anywhere] * 3, o...  5.33 us

profile of v7, /device:TPU:1, one launch (start us, length us, event | category | flops | bytes accessed | tf_op | source)
XLA Modules:
  0.0 68.9 jit_solution(13310784244872751113)
XLA Ops:
  0.6 62.9 %shard_map.76 = (f32[128,6912]{1,0:T(8,128)S(1)}, f32[128,6912]{1,0:T(8,128)S(1)}, bf16[4,128,6912]{2,1,0:T(8,128)(2,1)S(1)}) custom-call(bf16[1,128,6912]{2,1,0:T(8,128)(2,1)} %grads_ref.1, f32[1,128,6912]{2,1,0:T(8,128)} %mom_ref.1, s32[4,8,2,2,1728]{4,3,2,1,0:T(2,128)} %bitcast.1, f32[128,6912]{1,0:T(8,128)} %master_ref.1, ...), custom_call_target="tpu_custom_call" | custom-call | tf_op jit(solution)/shard_map/pallas_call | solution.py:552
  63.6 5.3 %shard_map.77 = (f32[1,128,6912]{2,1,0:T(8,128)}, f32[128,6912]{1,0:T(8,128)}, bf16[128,27648]{1,0:T(8,128)(2,1)}) custom-call(f32[128,6912]{1,0:T(8,128)S(1)} %get-tuple-element.6.fresh_ref, f32[128,6912]{1,0:T(8,128)S(1)} %get-tuple-element.7.update_ref, bf16[4,128,6912]{2,1,0:T(8,128)(2,1)S(1)} %get-tuple-element.8.slots_ref), custom_call_target="tpu_custom_call" | custom-call | tf_op jit(solution)/shard_map/pallas_call | solution.py:530
